TPU v7x, 128 devices: a whole 4x4x4 slice. The times are simulated.
128 devices in a mesh: ctx: 16 (over x_hi, y, core), exp: 8 (over x_lo, z).
Axes of the slice: x: 4 (x_hi: 2, x_lo: 2; x = x_hi * 2 + x_lo), y: 4, z: 4, core: 2. Of those that a mesh axis runs over, the one named last changes fastest.
Arguments:
- queries: bfloat16 [2048, 6144], P('ctx', 'exp'), may hold values from -96 to 96, as said below
- k_load: bfloat16 [2048, 1024], P('ctx', 'exp'), may hold values from -4 to 4
- v_load: bfloat16 [2048, 1024], P('ctx', 'exp'), may hold values from -5 to 5
- kv_scale: bfloat16 [128, 8, 2], P('ctx', 'exp'), may hold values from 0.5 to 2
- doc_ids: int32 [2048], P('ctx'), may hold values from 0 to 1, as said below
- residual_in: bfloat16 [2048, 6144], P(('ctx', 'exp')), may hold values from -3 to 3
- out_weight: bfloat16 [6144, 6144], P('exp', 'ctx'), may hold values from -0.15625 to 0.15625
- norm_gain: bfloat16 [6144], replicated, may hold values from 0.099609375 to 1.8984375
- w_gate: bfloat16 [8, 6144, 8192], P('exp', None, 'ctx'), may hold values from -0.078125 to 0.078125
- w_up: bfloat16 [8, 6144, 8192], P('exp', None, 'ctx'), may hold values from -0.078125 to 0.078125
- w_down: bfloat16 [8, 8192, 6144], P('exp', 'ctx'), may hold values from -0.125 to 0.125
- expert_ids: int32 [2048, 2], P(('ctx', 'exp')), may hold values from 0 to 7, all different within a row; in each aligned block of 16 rows (0 to 15, 16 to 31, ...) at most 8 rows name the same one
- route_logit: float32 [2048, 2], P(('ctx', 'exp')), may hold values from -6 to 6
Outputs:
- mixed: bfloat16 [2048, 6144], P(('ctx', 'exp'))
Inputs may be any that keep to these rules, and one draw needn't show every extreme that they name: `queries`: some rows may have every head equal to a multiple of its key head's row of k_load at the same token. `doc_ids`: never falling along the tokens. `expert_ids`: each row names two different experts; in each aligned block of 16 rows (the rows of one device) no expert is named by more than 8 rows, a bound that some block reaches.
All inputs are finite; a program needn't handle non-finite values.
Results may differ from a plain program's by a relative error of at most 0.03.
Values may be sent and summed in bfloat16 or wider, within the bound.
No kernel may reach another device: no remote copies, remote signals or barrier semaphores. Data moves between devices by JAX's collectives and lax.ppermute only.
A program may use at most 128 MiB of HBM per device.

v0:
```python
import functools
import math

import jax
import jax.numpy as jnp
from jax import lax
from jax.experimental import pallas as pl
from jax.experimental.pallas import tpu as pltpu
from jax.sharding import PartitionSpec as P

HQ = 48
KVH = 8
HD = 128
KBLK = 16
TOP = 2
CAP = 8
NY = 4
NE = 8
BOTH = ("ctx", "exp")
F32 = jnp.float32
BF16 = jnp.bfloat16


def partner(flip_x=0, step_y=0, flip_core=0):
    pairs = []
    for source in range(128):
        ctx, exp = divmod(source, NE)
        x_hi, y, core = ctx // 8, (ctx // 2) % NY, ctx % 2
        target = ((x_hi ^ flip_x) * 8 + ((y + step_y) % NY) * 2 + (core ^ flip_core)) * NE + exp
        pairs.append((source, target))
    return pairs


def flip_x(value):
    return lax.ppermute(value, BOTH, partner(flip_x=1))


def flip_core(value):
    return lax.ppermute(value, BOTH, partner(flip_core=1))


def from_y(value, step):
    return lax.ppermute(value, BOTH, partner(step_y=-step))


def slots_of(ids):
    order = jnp.arange(ids.shape[0], dtype=jnp.int32)
    same = (ids[:, None] == ids[None, :]) & (order[None, :] < order[:, None])
    return jnp.sum(same.astype(jnp.int32), axis=1)


def gather_y(own, axis):
    half = own.shape[axis] // 2
    above = from_y(own, 1)
    below = from_y(own, -1)
    far_lo = from_y(lax.slice_in_dim(below, 0, half, axis=axis), -1)
    far_hi = from_y(lax.slice_in_dim(above, half, 2 * half, axis=axis), 1)
    far = lax.concatenate([far_lo, far_hi], axis)
    return own, above, below, far


STEPS = (0, 1, -1, 2)
INNER = 2
OUTER = 4


def pack(k_load, v_load, scales, docs, out, keys, values, sems):
    copies = [
        pltpu.make_async_copy(k_load, keys, sems.at[0]),
        pltpu.make_async_copy(v_load, values, sems.at[1]),
    ]
    for copy in copies:
        copy.start()
    tok = keys.shape[0]
    block = lax.broadcasted_iota(jnp.int32, (tok, tok // KBLK), 0) // KBLK
    group = lax.broadcasted_iota(jnp.int32, (tok, tok // KBLK), 1)
    picked = jnp.where(block == group, 1.0, 0.0).astype(BF16)
    factor = lax.dot_general(
        picked, scales[...], (((1,), (1,)), ((), ())), preferred_element_type=F32
    )
    wide = jnp.broadcast_to(docs[...].astype(F32), (16, tok)).astype(BF16)
    out[tok:, :HD] = wide
    out[tok:, HD:] = wide
    copies[0].wait()
    out[:tok, :HD] = (keys[...].astype(F32) * factor[:, 0:1]).astype(BF16)
    copies[1].wait()
    out[:tok, HD:] = (values[...].astype(F32) * factor[:, 1:2]).astype(BF16)


def packed_keys(k_load, v_load, kv_scale, doc_ids):
    vmem, hbm = pl.BlockSpec(memory_space=pltpu.VMEM), pl.BlockSpec(memory_space=pl.ANY)
    tok = k_load.shape[0]
    return pl.pallas_call(
        pack,
        out_shape=jax.ShapeDtypeStruct((tok + 16, 2 * HD), BF16),
        in_specs=[hbm, hbm, vmem, vmem],
        out_specs=vmem,
        scratch_shapes=[
            pltpu.VMEM(k_load.shape, BF16),
            pltpu.VMEM(v_load.shape, BF16),
            pltpu.SemaphoreType.DMA((2,)),
        ],
        compiler_params=pltpu.CompilerParams(vmem_limit_bytes=8 * 2**20),
        cost_estimate=pl.CostEstimate(flops=200000, bytes_accessed=200000, transcendentals=0),
    )(k_load, v_load, kv_scale[:, 0, :].T, doc_ids[None, :])


def attend(start, queries, mine, other, out, scores):
    tok = queries.shape[0]
    heads = queries.shape[1] // HD
    stacked = jnp.concatenate([queries[:, i * HD : (i + 1) * HD] for i in range(heads)], 0)
    shards = [(mine, i) for i in range(mine.shape[0])] + [(other, i) for i in range(other.shape[0])]

    def docs_of(ref, i):
        return jnp.broadcast_to(ref[i, tok : tok + 16, :tok].astype(F32)[0:1], (tok, tok))

    own_docs = docs_of(mine, 0).T
    ahead = lax.broadcasted_iota(jnp.int32, (tok, tok), 0) - lax.broadcasted_iota(
        jnp.int32, (tok, tok), 1
    )
    best = jnp.full((heads * tok, tok), -3e38, F32)
    for j, (ref, i) in enumerate(shards):
        score = lax.dot_general(
            stacked, ref[i, :tok, :HD], (((1,), (1,)), ((), ())), preferred_element_type=F32
        ) * (1.0 / math.sqrt(HD))
        allowed = (ahead >= start[j] - start[0]) & (own_docs == docs_of(ref, i))
        bias = jnp.where(allowed, 0.0, -1e30)
        score = score + jnp.concatenate([bias] * heads, 0)
        scores[:, j * tok : (j + 1) * tok] = score
        best = jnp.maximum(best, score)
    best = jnp.max(best, axis=1, keepdims=True)
    total = jnp.zeros((heads * tok, tok), F32)
    accum = jnp.zeros((heads * tok, HD), F32)
    for j, (ref, i) in enumerate(shards):
        expo = jnp.exp(scores[:, j * tok : (j + 1) * tok] - best)
        total = total + expo
        accum = accum + jnp.dot(
            expo.astype(BF16), ref[i, :tok, HD:], preferred_element_type=F32
        )
    result = (accum / jnp.sum(total, axis=1, keepdims=True)).astype(BF16)
    for i in range(heads):
        out[:, i * HD : (i + 1) * HD] = result[i * tok : (i + 1) * tok]


def attention(queries, mine, other, place):
    x_hi, y, core = place
    tok = queries.shape[0]
    start = []
    for c in (core, 1 - core):
        for xh in (x_hi, 1 - x_hi):
            for step in STEPS:
                start.append(((xh * NY + (y + step) % NY) * 2 + c) * tok)
    vmem = pl.BlockSpec(memory_space=pltpu.VMEM)
    return pl.pallas_call(
        attend,
        out_shape=jax.ShapeDtypeStruct(queries.shape, BF16),
        in_specs=[pl.BlockSpec(memory_space=pltpu.SMEM), vmem, vmem, vmem],
        out_specs=vmem,
        scratch_shapes=[pltpu.VMEM((queries.size // HD, 16 * tok), F32)],
        compiler_params=pltpu.CompilerParams(vmem_limit_bytes=24 * 2**20),
        cost_estimate=pl.CostEstimate(
            flops=4 * queries.size * 16 * tok, bytes_accessed=1600000, transcendentals=1600000
        ),
    )(jnp.stack(start).astype(jnp.int32), queries, mine, other)


def project(block, across, near, far, near_other, far_other, out):
    step, half = pl.program_id(0), pl.num_programs(0) // 2
    rows = out.shape[1] // 2
    both = jnp.concatenate(
        [block[...].reshape(NE, 1, rows, -1), across[...].reshape(NE, 1, rows, -1)], 1
    ).reshape(NE * 2 * rows, -1)

    def store(weight):
        product = jnp.dot(both, weight[...], preferred_element_type=F32)
        out[...] = product.astype(BF16).reshape(out.shape)

    pl.when(step < half - 1)(lambda: store(near))
    pl.when(step == half - 1)(lambda: store(far))
    pl.when((step >= half) & (step < 2 * half - 1))(lambda: store(near_other))
    pl.when(step == 2 * half - 1)(lambda: store(far_other))


def projection(block, across, near, far, near_other, far_other, rows):
    depth, part = far.shape
    whole = pl.BlockSpec(block.shape, lambda i: (0, 0))
    single = pl.BlockSpec((depth, part), lambda i: (0, 0))
    return pl.pallas_call(
        project,
        grid=(2 * NY,),
        out_shape=jax.ShapeDtypeStruct((NE, 2 * rows, 2 * NY * part), BF16),
        in_specs=[
            whole,
            whole,
            pl.BlockSpec((depth, part), lambda i: (0, jnp.minimum(i, NY - 2))),
            single,
            pl.BlockSpec((depth, part), lambda i: (0, jnp.clip(i - NY, 0, NY - 2))),
            single,
        ],
        out_specs=pl.BlockSpec((NE, 2 * rows, part), lambda i: (0, 0, i)),
        compiler_params=pltpu.CompilerParams(vmem_limit_bytes=24 * 2**20),
        cost_estimate=pl.CostEstimate(
            flops=16 * block.size * NY * part, bytes_accessed=6500000, transcendentals=0
        ),
    )(block, across, near, far, near_other, far_other)


def sum_and_sort(shift, terms, res_own, res_across, place, resid, outgoing):
    y, core = shift[0], shift[1]
    total = terms[0].astype(F32)
    for i in range(1, NE):
        total = total + terms[i].astype(F32)
    piece = total.shape[1] // (2 * NY)
    parts = [
        [total[:, (c * NY + i) * piece : (c * NY + i + 1) * piece] for i in (0, 1, 3, 2)]
        for c in range(2)
    ]
    for bit in (1, 2):
        moved = (y & bit) != 0
        parts = [
            [jnp.where(moved, row[(i - bit) % NY], row[i]) for i in range(NY)] for row in parts
        ]
    residual = jnp.concatenate([res_own[...], res_across[...]], 0).astype(F32)
    sums = []
    for i in range(NY):
        for c in range(2):
            value = jnp.where(core == 0, parts[c][i], parts[1 - c][i])
            columns = slice((2 * i + c) * piece, (2 * i + c + 1) * piece)
            sums.append((residual[:, columns] + value).astype(BF16))
    summed = jnp.concatenate(sums, 1)
    resid[...] = summed
    row = lax.broadcasted_iota(jnp.int32, (outgoing.shape[0], summed.shape[0]), 0)
    chosen = (row == place[0:1, :]) | (row == place[1:2, :])
    chosen = jnp.where(chosen, 1.0, 0.0).astype(BF16)
    outgoing[...] = jnp.dot(chosen, summed, preferred_element_type=F32).astype(BF16)


def residual_rows(y, core, terms, res_own, res_across, place):
    vmem = pl.BlockSpec(memory_space=pltpu.VMEM)
    rows, half = terms.shape[1:]
    return pl.pallas_call(
        sum_and_sort,
        out_shape=[
            jax.ShapeDtypeStruct((rows, half), BF16),
            jax.ShapeDtypeStruct((NE * 2 * CAP, half), BF16),
        ],
        in_specs=[pl.BlockSpec(memory_space=pltpu.SMEM)] + [vmem] * 4,
        out_specs=[vmem] * 2,
        compiler_params=pltpu.CompilerParams(vmem_limit_bytes=16 * 2**20),
        cost_estimate=pl.CostEstimate(
            flops=26000000, bytes_accessed=2600000, transcendentals=0
        ),
    )(jnp.stack([y, core]), terms, res_own, res_across, place)


def add_products(blocks, gain, weights, products, square):
    block = jnp.concatenate([b[...] for b in blocks], 0).astype(F32)
    scaled = (block * gain[...].astype(F32)).astype(BF16)
    squares = block * block
    lanes = square.shape[1]
    for i in range(squares.shape[1] // lanes):
        square[...] += squares[:, i * lanes : (i + 1) * lanes]
    for i, weight in enumerate(weights):
        products[i] += jnp.dot(scaled, weight[...], preferred_element_type=F32)


def begin(which, near, above, below, far, gain, g0, g1, u0, u1, products, square):
    @pl.when(pl.program_id(0) == 0)
    def _():
        products[...] = jnp.zeros_like(products)
        square[...] = jnp.zeros_like(square)

    add_products((near, above, below, far), gain, (g0, g1, u0, u1), products, square)


def finish(
    which, near, above, below, far, gain, before, squares, *refs
):
    weights, (own, other), (out, *firsts) = refs[:4], refs[4:6], refs[6:10]
    scaled, inner, outer, inner_sem, outer_sem = refs[10:]
    half = near.shape[1]
    width, unit = own.shape[1], own.shape[0]
    deep, wide = half // INNER, width // OUTER
    start = which[0] * half

    def inner_copy(i, part):
        rows = pl.ds(pl.multiple_of(start + part * deep, deep), deep)
        return pltpu.make_async_copy(
            weights[i].at[rows], inner.at[i, pl.ds(part * deep, deep)], inner_sem.at[i, part]
        )

    def outer_copy(i, part):
        columns = pl.ds(part * wide, wide)
        return pltpu.make_async_copy(
            (own, other)[i].at[:, columns], outer.at[i, :, columns], outer_sem.at[i, part]
        )

    for part in range(INNER):
        for i in range(4):
            inner_copy(i, part).start()
    for part in range(OUTER):
        for i in range(2):
            outer_copy(i, part).start()

    rows = near.shape[0]
    total = []
    for k, ref in enumerate((near, above, below, far)):
        block = ref[...].astype(F32)
        scaled[k * rows : (k + 1) * rows] = (block * gain[...].astype(F32)).astype(BF16)
        total.append(jnp.sum(block * block, axis=1, keepdims=True))
    square = jnp.concatenate(total, 0) + jnp.sum(squares[...], axis=1, keepdims=True)
    scale = lax.rsqrt(square / width + 1e-05)
    products = [before[i] for i in range(4)]
    for part in range(INNER):
        span = slice(part * deep, (part + 1) * deep)
        for i in range(4):
            inner_copy(i, part).wait()
            products[i] = products[i] + jnp.dot(
                scaled[:, span], inner[i, span], preferred_element_type=F32
            )
    first = which[1] == 0
    for i in range(2):
        gate = products[i] * scale
        hidden = gate / (1.0 + jnp.exp(-gate)) * (products[2 + i] * scale)
        hidden = hidden.reshape(NY, NE, 2, CAP, unit)
        even = hidden[:, :, 0].reshape(NY, NE * CAP, unit).astype(BF16)
        odd = hidden[:, :, 1].reshape(NY, NE * CAP, unit).astype(BF16)
        columns = slice(i * unit, (i + 1) * unit)
        out[0, :, :, columns] = jnp.where(first, even, odd)
        out[1, :, :, columns] = jnp.where(first, odd, even)
    sent = out[1, 1:].reshape(3 * NE * CAP, 2 * unit)
    for part in range(OUTER):
        columns = slice(part * wide, (part + 1) * wide)
        for i in range(2):
            outer_copy(i, part).wait()
        product = jnp.dot(sent[:, :unit], outer[0, :, columns], preferred_element_type=F32)
        product += jnp.dot(sent[:, unit:], outer[1, :, columns], preferred_element_type=F32)
        for k, ref in enumerate(firsts):
            ref[:, columns] = product[k * NE * CAP : (k + 1) * NE * CAP].astype(BF16)


def expert_rest(which, blocks, gain, before, weights, own, other):
    rows, half = blocks[0].shape
    unit, width = own.shape
    vmem, hbm = pl.BlockSpec(memory_space=pltpu.VMEM), pl.BlockSpec(memory_space=pl.ANY)
    return pl.pallas_call(
        finish,
        out_shape=[jax.ShapeDtypeStruct((2, NY, rows // 2, 2 * unit), BF16)]
        + [jax.ShapeDtypeStruct((rows // 2, width), BF16)] * 3,
        in_specs=[pl.BlockSpec(memory_space=pltpu.SMEM)] + [vmem] * (NY + 3) + [hbm] * 6,
        out_specs=[vmem] * 4,
        scratch_shapes=[
            pltpu.VMEM((NY * rows, half), BF16),
            pltpu.VMEM((4, half, unit), BF16),
            pltpu.VMEM((2, unit, width), BF16),
            pltpu.SemaphoreType.DMA((4, INNER)),
            pltpu.SemaphoreType.DMA((2, OUTER)),
        ],
        compiler_params=pltpu.CompilerParams(vmem_limit_bytes=42 * 2**20),
        cost_estimate=pl.CostEstimate(
            flops=12 * NY * rows * half * unit, bytes_accessed=26000000, transcendentals=600000
        ),
    )(which, *blocks, gain, *before, *weights, own, other)


def expert_in(which, blocks, gain, weights):
    rows, half = blocks[0].shape
    unit = weights[0].shape[1]
    part = 1024
    steps = half // part
    total = NY * rows
    sums = [(4, total, unit), (total, 128)]
    return pl.pallas_call(
        begin,
        grid_spec=pltpu.PrefetchScalarGridSpec(
            num_scalar_prefetch=1,
            grid=(steps,),
            in_specs=[pl.BlockSpec((rows, part), lambda k, w: (0, k))] * NY
            + [pl.BlockSpec((1, part), lambda k, w: (0, w[0] * steps + k))]
            + [pl.BlockSpec((part, unit), lambda k, w: (w[0] * steps + k, 0))] * 4,
            out_specs=[
                pl.BlockSpec(sums[0], lambda k, w: (0, 0, 0)),
                pl.BlockSpec(sums[1], lambda k, w: (0, 0)),
            ],
        ),
        out_shape=[jax.ShapeDtypeStruct(shape, F32) for shape in sums],
        compiler_params=pltpu.CompilerParams(vmem_limit_bytes=40 * 2**20),
        cost_estimate=pl.CostEstimate(
            flops=8 * total * half * unit, bytes_accessed=16000000, transcendentals=0
        ),
    )(which, *blocks, gain, *weights)


def down_rows(rows, split, hidden, own, other, *outs):
    units = own.shape[0]
    stacked = jnp.concatenate([hidden[a, k] for a, k in rows], 0)
    product = jnp.dot(stacked[:, :units], own[...], preferred_element_type=F32) + jnp.dot(
        stacked[:, units:], other[...], preferred_element_type=F32
    )
    product = product.astype(BF16)
    height = hidden.shape[2]
    step, steps = pl.program_id(0), pl.num_programs(0)
    at = 0
    for i in range(len(rows)):
        piece = product[i * height : (i + 1) * height]
        if i in split:
            for want, ref in ((step < steps // 2, outs[at]), (step >= steps // 2, outs[at + 1])):

                @pl.when(want)
                def _(ref=ref, piece=piece):
                    ref[...] = piece

            at += 2
        else:
            outs[at][...] = piece
            at += 1


def expert_out_part(hidden, own, other, rows, split=()):
    height, (units, width) = hidden.shape[2], own.shape
    part = 1024
    steps = width // part
    shapes, specs = [], []
    for i in range(len(rows)):
        if i in split:
            shapes += [jax.ShapeDtypeStruct((height, width // 2), BF16)] * 2
            specs += [
                pl.BlockSpec((height, part), lambda n: (0, jnp.minimum(n, steps // 2 - 1))),
                pl.BlockSpec((height, part), lambda n: (0, jnp.maximum(n - steps // 2, 0))),
            ]
        else:
            shapes.append(jax.ShapeDtypeStruct((height, width), BF16))
            specs.append(pl.BlockSpec((height, part), lambda n: (0, n)))
    return pl.pallas_call(
        functools.partial(down_rows, rows, split),
        grid=(steps,),
        out_shape=shapes,
        in_specs=[
            pl.BlockSpec(hidden.shape, lambda n: (0, 0, 0, 0)),
            pl.BlockSpec((units, part), lambda n: (0, n)),
            pl.BlockSpec((units, part), lambda n: (0, n)),
        ],
        out_specs=specs,
        compiler_params=pltpu.CompilerParams(vmem_limit_bytes=32 * 2**20),
        cost_estimate=pl.CostEstimate(
            flops=4 * len(rows) * height * units * width, bytes_accessed=15000000, transcendentals=0
        ),
    )(hidden, own, other)


def per_device(
    queries,
    k_load,
    v_load,
    kv_scale,
    doc_ids,
    residual_in,
    out_weight,
    norm_gain,
    w_gate,
    w_up,
    w_down,
    expert_ids,
    route_logit,
):
    ctx = lax.axis_index("ctx")
    x_hi, y, core = ctx // 8, (ctx // 2) % NY, ctx % 2
    tok = queries.shape[0]
    rows = residual_in.shape[0]
    width = residual_in.shape[1]
    half = width // 2
    gate_own, up_own, down_own = w_gate[0], w_up[0], w_down[0]

    ids = expert_ids.reshape(-1)
    key_value = packed_keys(k_load, v_load, kv_scale, doc_ids)
    out_weight, key_value = lax.optimization_barrier((out_weight, key_value))
    res_send = lax.dynamic_slice_in_dim(residual_in, (1 - x_hi) * half, half, 1)
    column = jnp.stack([key_value] + [from_y(key_value, step) for step in STEPS[1:]])
    near_pieces = [from_y(out_weight, 1), from_y(out_weight, -1)]
    mine = jnp.concatenate([column, flip_x(column)], 0)
    mine, *near_pieces = lax.optimization_barrier((mine, *near_pieces))
    other = flip_core(mine)
    cut = out_weight.shape[0] // 2
    far_halves = from_y(near_pieces[1][:cut], -1), from_y(near_pieces[0][cut:], 1)
    attn = attention(queries, mine, other, (x_hi, y, core))

    attn_across = flip_x(attn)
    near_mine = jnp.concatenate([out_weight, *near_pieces], 1)
    near_other = flip_core(near_mine)
    near_other, attn_across, far_lo, far_hi, res_send, early_ids = lax.optimization_barrier(
        (near_other, attn_across, *far_halves, res_send, ids)
    )
    far_mine = jnp.concatenate([far_lo, far_hi], 0)
    far_other = flip_core(far_mine)
    far_other, gate_own, up_own, down_own = lax.optimization_barrier(
        (far_other, gate_own, up_own, down_own)
    )
    res_across, across_ids = flip_x(res_send), flip_x(early_ids)
    partial = projection(
        attn, attn_across, near_mine, far_mine, near_other, far_other, rows
    )
    terms = lax.all_to_all(partial, "exp", split_axis=0, concat_axis=0, tiled=True)
    res_own = lax.dynamic_slice_in_dim(residual_in, x_hi * half, half, 1)

    slots_own = slots_of(ids)
    slots_across = slots_of(across_ids)
    place = jnp.concatenate(
        [
            (ids * 2 + x_hi) * CAP + slots_own,
            (across_ids * 2 + 1 - x_hi) * CAP + slots_across,
        ]
    ).reshape(2 * rows, TOP)
    resid, outgoing = residual_rows(y, core, terms, res_own, res_across, place.T)
    gate_other, up_other = flip_core(gate_own), flip_core(up_own)
    outgoing, gate_other, up_other = lax.optimization_barrier((outgoing, gate_other, up_other))
    arrived = lax.all_to_all(
        outgoing.reshape(NE, 2 * CAP, half), "exp", split_axis=0, concat_axis=0, tiled=True
    ).reshape(NE * 2 * CAP, half)
    down_other = flip_core(down_own)

    near, above, below, far = gather_y(arrived, 0)
    near_x = flip_x(near)
    above_x, below_x = from_y(near_x, 1), from_y(near_x, -1)
    far_x = flip_x(far)
    resid_across = flip_x(resid[rows:])
    gain = norm_gain.reshape(1, width)
    weights = (gate_own, gate_other, up_own, up_other)
    before = expert_in(x_hi[None], (near, above, below, far), gain, weights)
    *before, down_other = lax.optimization_barrier((*before, down_other))
    there = lax.dynamic_slice_in_dim(gain, (1 - x_hi) * half, half, 1)

    hidden, to_above, to_below, to_far = expert_rest(
        jnp.stack([1 - x_hi, x_hi]),
        (near_x, above_x, below_x, far_x),
        there,
        before,
        weights,
        down_own,
        down_other,
    )
    from_below = from_y(to_above, -1)
    from_above = from_y(to_below, 1)
    from_far = flip_x(to_far)
    above_lo, above_hi, below_lo, below_hi, cross, far_own, own = expert_out_part(
        hidden, down_own, down_other, ((0, 1), (0, 2), (1, 0), (0, 3), (0, 0)), (0, 1)
    )

    def added(*terms):
        return sum(t.astype(F32) for t in terms).astype(BF16)

    far_lo = from_y(added(far_own[:, :half], from_far[:, :half]), -1)
    far_hi = from_y(added(far_own[:, half:], from_far[:, half:]), 1)
    cross, above_hi, below_lo = lax.optimization_barrier(
        (added(cross, from_below, from_above), above_hi, below_lo)
    )
    from_cross = flip_x(cross)
    free_below = from_y(above_hi, -1)
    free_above = from_y(below_lo, 1)
    last_below = from_y(added(above_lo, far_lo), -1)
    last_above = from_y(added(below_hi, far_hi), 1)
    from_cross, last_below, last_above = lax.optimization_barrier(
        (from_cross, last_below, last_above)
    )
    expert_out = jnp.concatenate(
        [
            added(own[:, :half], from_cross[:, :half], free_above, last_below),
            added(own[:, half:], from_cross[:, half:], free_below, last_above),
        ],
        1,
    )

    returned = lax.all_to_all(
        expert_out.reshape(NE, CAP, width), "exp", split_axis=0, concat_axis=0, tiled=True
    ).reshape(NE * CAP, width)
    route = jax.nn.softmax(route_logit, axis=1)
    position = (ids * CAP + slots_own).reshape(rows, TOP)
    column = jnp.arange(NE * CAP, dtype=jnp.int32)[None, :]
    halves = [resid[:rows], resid_across]
    own_row = jnp.where(
        x_hi == 0, jnp.concatenate(halves, 1), jnp.concatenate(halves[::-1], 1)
    ).astype(F32)
    for k in range(TOP):
        chosen = (position[:, k : k + 1] == column).astype(BF16)
        own_row = own_row + route[:, k : k + 1] * jnp.dot(
            chosen, returned, preferred_element_type=F32
        )
    return own_row.astype(BF16)


def solution(mesh):
    return jax.shard_map(
        per_device,
        mesh=mesh,
        in_specs=(
            P("ctx", "exp"),
            P("ctx", "exp"),
            P("ctx", "exp"),
            P("ctx", "exp", None),
            P("ctx"),
            P(("ctx", "exp"), None),
            P("exp", "ctx"),
            P(),
            P("exp", None, "ctx"),
            P("exp", None, "ctx"),
            P("exp", "ctx", None),
            P(("ctx", "exp"), None),
            P(("ctx", "exp"), None),
        ),
        out_specs=P(("ctx", "exp"), None),
        check_vma=False,
    )
```

profile of v0, /device:TPU:0, one launch (start us, length us, event | category | flops | bytes accessed | tf_op | source)
XLA Modules:
  0.0 223.0 jit_solution(16904638268470850210)
XLA Ops:
  0.0 0.8 copy-done.2
  0.8 0.8 copy-done.3
  1.5 0.7 copy-done.4
  2.2 0.7 copy-done.5
  2.8 0.4 shard_map.127
  3.2 3.2 %collective-permute-start = (bf16[144,256]{1,0:T(8,128)(2,1)S(1)}, bf16[144,256]{1,0:T(8,128)(2,1)S(1)}, u32[]{:S(2)}, u32[]{:S(2)}) collective-permute-start(bf16[144,256]{1,0:T(8,128)(2,1)S(1)} %shard_map.127), channel_id=1, source_target_pairs={{0,48},{1,49},{2,50},{3,51},{4,52},{5,53},{6,54},{7,55},{8,56},{9,... | collective-permute-start | bytes 221192 | tf_op jit(solution)/shard_map/ppermute | solution.py:43
  6.4 2.2 collective-permute-start.2
  8.6 1.1 collective-permute-start.4
  9.6 1.0 collective-permute-start.5
  10.6 1.2 constant_dynamic-update-slice_fusion.7
  11.8 1.4 collective-permute-done.1
  13.2 3.1 %collective-permute-start.3 = (bf16[4,144,256]{2,1,0:T(8,128)(2,1)S(1)}, bf16[4,144,256]{2,1,0:T(8,128)(2,1)S(1)}, u32[]{:S(2)}, u32[]{:S(2)}) collective-permute-start(bf16[4,144,256]{2,1,0:T(8,128)(2,1)S(1)} %pad_maximum_fusion), channel_id=1, source_target_pairs={{0,64},{1,65},{2,66},{3,67},{4,68},{5,69},{6,70},{7,71},{8,72},{9,... | collective-permute-start | bytes 884744 | tf_op jit(solution)/shard_map/ppermute | solution.py:35
  16.3 5.6 %collective-permute-done.3 = bf16[4,144,256]{2,1,0:T(8,128)(2,1)S(1)} collective-permute-done((bf16[4,144,256]{2,1,0:T(8,128)(2,1)S(1)}, bf16[4,144,256]{2,1,0:T(8,128)(2,1)S(1)}, u32[]{:S(2)}, u32[]{:S(2)}) %collective-permute-start.3) | collective-permute-done | bytes 294944 | tf_op jit(solution)/shard_map/ppermute | solution.py:35
  21.9 2.6 %collective-permute-done.4 = bf16[768,384]{1,0:T(8,128)(2,1)S(1)} collective-permute-done((bf16[768,384]{1,0:T(8,128)(2,1)}, bf16[768,384]{1,0:T(8,128)(2,1)S(1)}, u32[]{:S(2)}, u32[]{:S(2)}) %collective-permute-start.4) | collective-permute-done | bytes 589856 | tf_op jit(solution)/shard_map/ppermute | solution.py:43
  24.5 1.0 collective-permute-done.5
  25.9 0.5 copy-done.8
  26.7 1.0 slice.55
  27.7 1.0 slice.54
  28.7 2.2 collective-permute-start.10
  30.9 5.2 %shard_map.128.block = bf16[128,768]{1,0:T(8,128)(2,1)S(1)} custom-call(s32[16]{0:T(128)S(1)} %stack.103.start, bf16[128,768]{1,0:T(8,128)(2,1)S(1)} %copy-done.6, bf16[8,144,256]{2,1,0:T(8,128)(2,1)S(1)} %constant_dynamic-update-slice_fusion.mine, bf16[8,144,256]{2,1,0:T(8,128)(2,1)S(1)} %collective-permute-done.6.other), custom_call_target="tpu_custom_call" | custom-call | flops 805306368 | bytes 1600000 | tf_op jit(solution)/shard_map/pallas_call | solution.py:154
  36.1 3.1 %collective-permute-start.8 = (bf16[128,768]{1,0:T(8,128)(2,1)S(1)}, bf16[128,768]{1,0:T(8,128)(2,1)S(1)}, u32[]{:S(2)}, u32[]{:S(2)}) collective-permute-start(bf16[128,768]{1,0:T(8,128)(2,1)S(1)} %shard_map.128.block), channel_id=1, source_target_pairs={{0,64},{1,65},{2,66},{3,67},{4,68},{5,69},{6,70},{7,71},{8,72},{9,... | collective-permute-start | bytes 589832 | tf_op jit(solution)/shard_map/ppermute | solution.py:35
  39.2 1.7 collective-permute-done.9
  40.9 3.5 %collective-permute-done.8.across = bf16[128,768]{1,0:T(8,128)(2,1)S(1)} collective-permute-done((bf16[128,768]{1,0:T(8,128)(2,1)S(1)}, bf16[128,768]{1,0:T(8,128)(2,1)S(1)}, u32[]{:S(2)}, u32[]{:S(2)}) %collective-permute-start.8) | collective-permute-done | bytes 196640 | tf_op jit(solution)/shard_map/ppermute | solution.py:35
  44.6 2.0 collective-permute-done.11.far_other
  46.7 0.4 collective-permute-start.16
  47.2 6.7 %shard_map.129 = bf16[8,32,3072]{2,1,0:T(8,128)(2,1)} custom-call(bf16[128,768]{1,0:T(8,128)(2,1)S(1)} %shard_map.128.block, bf16[128,768]{1,0:T(8,128)(2,1)S(1)} %collective-permute-done.8.across, bf16[768,1152]{1,0:T(8,128)(2,1)S(1)} %constant_dynamic-update-slice_fusion.5.near, bf16[768,384]{1,0:T(8,128)(2,1)S(1)} %constant_dynamic-update-slice_fusion.8.far, ...), custom_call_target="tpu_custom_call" | custom-call | flops 2415919104 | bytes 6500000 | tf_op jit(solution)/shard_map/pallas_call | solution.py:188
  53.9 6.3 %all-to-all-start = ((bf16[8,32,3072]{2,1,0:T(8,128)(2,1)}), bf16[8,32,3072]{2,1,0:T(8,128)(2,1)S(1)}, u32[]{:S(2)}, u32[]{:S(2)}) async-start(bf16[8,32,3072]{2,1,0:T(8,128)(2,1)} %shard_map.129), calls=%async_computation | async-start | bytes 3145728 | tf_op jit(solution)/shard_map/all_to_all | solution.py:502
  60.5 2.8 %collective-permute-start.13 = (s32[32]{0:T(128)S(1)}, s32[32]{0:T(128)S(1)}, u32[]{:S(2)}, u32[]{:S(2)}) collective-permute-start(s32[32]{0:T(128)S(1)} %reshape.31), channel_id=1, source_target_pairs={{0,64},{1,65},{2,66},{3,67},{4,68},{5,69},{6,70},{7,71},{8,72},{9,... | collective-permute-start | bytes 392 | tf_op jit(solution)/shard_map/ppermute | solution.py:35
  63.3 0.8 collective-permute-start.12
  64.1 17.4 %collective-permute-done.13 = s32[32]{0:T(128)S(1)} collective-permute-done((s32[32]{0:T(128)S(1)}, s32[32]{0:T(128)S(1)}, u32[]{:S(2)}, u32[]{:S(2)}) %collective-permute-start.13) | collective-permute-done | bytes 160 | tf_op jit(solution)/shard_map/ppermute | solution.py:35
  81.9 1.1 collective-permute-done.12.res_across
  83.0 1.1 shard_map.130
  84.2 16.9 %all_to_all.15 = bf16[8,16,3072]{2,1,0:T(8,128)(2,1)S(1)} all-to-all(bf16[8,16,3072]{2,1,0:T(8,128)(2,1)S(1)} %bitcast.66), channel_id=1, replica_groups=mesh['ctx'=16,'exp'=8] {'exp'}, dimensions={0} | all-to-all | bytes 1572864 | tf_op jit(solution)/shard_map/all_to_all | solution.py:516
  101.1 0.3 collective-permute-start.20
  101.4 2.9 %collective-permute-start.22 = (bf16[128,3072]{1,0:T(8,128)(2,1)S(1)}, bf16[128,3072]{1,0:T(8,128)(2,1)S(1)}, u32[]{:S(2)}, u32[]{:S(2)}) collective-permute-start(bf16[128,3072]{1,0:T(8,128)(2,1)S(1)} %bitcast.63), channel_id=1, source_target_pairs={{0,48},{1,49},{2,50},{3,51},{4,52},{5,53},{6,54},{7,55},{8,56},{9,... | collective-permute-start | bytes 2359304 | tf_op jit(solution)/shard_map/ppermute | solution.py:43
  104.3 2.0 collective-permute-start.17
  106.3 12.8 %collective-permute-done.20.below = bf16[128,3072]{1,0:T(8,128)(2,1)S(1)} collective-permute-done((bf16[128,3072]{1,0:T(8,128)(2,1)S(1)}, bf16[128,3072]{1,0:T(8,128)(2,1)S(1)}, u32[]{:S(2)}, u32[]{:S(2)}) %collective-permute-start.20) | collective-permute-done | bytes 786464 | tf_op jit(solution)/shard_map/ppermute | solution.py:43
  119.3 3.3 %collective-permute-start.23 = (bf16[64,3072]{1,0:T(8,128)(2,1)S(1)}, bf16[64,3072]{1,0:T(8,128)(2,1)S(1)}, u32[]{:S(2)}, u32[]{:S(2)}) collective-permute-start(bf16[64,3072]{1,0:T(8,128)(2,1)S(1)} %slice.73), channel_id=1, source_target_pairs={{0,48},{1,49},{2,50},{3,51},{4,52},{5,53},{6,54},{7,55},{8,56},{9,... | collective-permute-start | bytes 1179656 | tf_op jit(solution)/shard_map/ppermute | solution.py:43
  122.6 1.3 collective-permute-start.18
  123.9 0.7 collective-permute-start.19
  124.6 7.9 %collective-permute-done.21 = bf16[64,3072]{1,0:T(8,128)(2,1)S(1)} collective-permute-done((bf16[64,3072]{1,0:T(8,128)(2,1)S(1)}, bf16[64,3072]{1,0:T(8,128)(2,1)S(1)}, u32[]{:S(2)}, u32[]{:S(2)}) %collective-permute-start.21) | collective-permute-done | bytes 393248 | tf_op jit(solution)/shard_map/ppermute | solution.py:43
  132.6 2.1 collective-permute-start.24
  134.8 2.8 %copy-done = bf16[1,6144,512]{2,1,0:T(8,128)(2,1)S(1)} copy-done((bf16[1,6144,512]{2,1,0:T(8,128)(2,1)S(1)}, bf16[1,6144,512]{2,1,0:T(8,128)(2,1)}, u32[]{:S(2)}) %copy-start) | copy-done | bytes 6291480
  137.6 9.7 %shard_map.131 = (f32[4,512,512]{2,1,0:T(8,128)S(1)}, f32[512,128]{1,0:T(8,128)S(1)}) custom-call(s32[1]{0:T(128)} %bitcast.32.which, bf16[128,3072]{1,0:T(8,128)(2,1)S(1)} %bitcast.65, bf16[128,3072]{1,0:T(8,128)(2,1)S(1)} %collective-permute-done.22.above, bf16[128,3072]{1,0:T(8,128)(2,1)S(1)} %collective-permute-done.20.below, ...), custom_call_target="tpu_custom_call" | custom-call | flops 6442450944 | bytes 16000000 | tf_op jit(solution)/shard_map/pallas_call | solution.py:373
  147.3 15.4 %shard_map.132 = (bf16[2,4,64,1024]{3,2,1,0:T(8,128)(2,1)S(1)}, bf16[64,6144]{1,0:T(8,128)(2,1)S(1)}, bf16[64,6144]{1,0:T(8,128)(2,1)S(1)}, bf16[64,6144]{1,0:T(8,128)(2,1)}) custom-call(s32[2]{0:T(128)S(1)} %pad_add_fusion.1.which, bf16[128,3072]{1,0:T(8,128)(2,1)S(1)} %collective-permute-done.17.near, bf16[128,3072]{1,0:T(8,128)(2,1)S(1)} %collective-permute-done.18.above, ...), custom_call_target="tpu_custom_call" | custom-call | flops 9663676416 | bytes 26000000 | tf_op jit(solution)/shard_map/pallas_call | solution.py:346
  162.8 1.6 collective-permute-start.29
  164.4 0.8 collective-permute-start.26
  165.2 2.8 %collective-permute-start.27 = (bf16[64,6144]{1,0:T(8,128)(2,1)S(1)}, bf16[64,6144]{1,0:T(8,128)(2,1)S(1)}, u32[]{:S(2)}, u32[]{:S(2)}) collective-permute-start(bf16[64,6144]{1,0:T(8,128)(2,1)S(1)} %get-tuple-element.76), channel_id=1, source_target_pairs={{0,48},{1,49},{2,50},{3,51},{4,52},{5,53},{6,54},{7,55},{8,56},{9,... | collective-permute-start | bytes 2359304 | tf_op jit(solution)/shard_map/ppermute | solution.py:43
  168.1 2.8 %copy-done.1 = bf16[1,512,6144]{2,1,0:T(8,128)(2,1)S(1)} copy-done((bf16[1,512,6144]{2,1,0:T(8,128)(2,1)S(1)}, bf16[1,512,6144]{2,1,0:T(8,128)(2,1)}, u32[]{:S(2)}) %copy-start.1) | copy-done | bytes 6291480
  170.9 8.1 %shard_map.133 = (bf16[64,3072]{1,0:T(8,128)(2,1)S(1)}, bf16[64,3072]{1,0:T(8,128)(2,1)S(1)}, bf16[64,3072]{1,0:T(8,128)(2,1)S(1)}, bf16[64,3072]{1,0:T(8,128)(2...) custom-call(bf16[2,4,64,1024]{3,2,1,0:T(8,128)(2,1)S(1)} %get-tuple-element.72.hid, ...), custom_call_target="tpu_custom_call" | custom-call | flops 4026531840 | bytes 15000000 | tf_op jit(solution)/shard_map/pallas_call | solution.py:434
  178.9 1.3 add_convert_fusion.4
  180.2 1.8 collective-permute-start.32
  182.6 2.1 collective-permute-start.28
  184.7 2.9 %collective-permute-start.34 = (bf16[64,3072]{1,0:T(8,128)(2,1)S(1)}, bf16[64,3072]{1,0:T(8,128)(2,1)S(1)}, u32[]{:S(2)}, u32[]{:S(2)}) collective-permute-start(bf16[64,3072]{1,0:T(8,128)(2,1)S(1)} %get-tuple-element.85), channel_id=1, source_target_pairs={{0,48},{1,49},{2,50},{3,51},{4,52},{5,53},{6,54},{7,55},{8,56},{9,... | collective-permute-start | bytes 1179656 | tf_op jit(solution)/shard_map/ppermute | solution.py:43
  187.7 4.7 %collective-permute-done.32 = bf16[64,3072]{1,0:T(8,128)(2,1)S(1)} collective-permute-done((bf16[64,3072]{1,0:T(8,128)(2,1)S(1)}, bf16[64,3072]{1,0:T(8,128)(2,1)S(1)}, u32[]{:S(2)}, u32[]{:S(2)}) %collective-permute-start.32) | collective-permute-done | bytes 393248 | tf_op jit(solution)/shard_map/ppermute | solution.py:43
  192.5 3.0 %collective-permute-start.33 = (bf16[64,3072]{1,0:T(8,128)(2,1)S(1)}, bf16[64,3072]{1,0:T(8,128)(2,1)S(1)}, u32[]{:S(2)}, u32[]{:S(2)}) collective-permute-start(bf16[64,3072]{1,0:T(8,128)(2,1)S(1)} %add_convert_fusion.3), channel_id=1, source_target_pairs={{0,48},{1,49},{2,50},{3,51},{4,52},{5,53},{6,54},{7,55},{8,56},{9,... | collective-permute-start | bytes 1179656 | tf_op jit(solution)/shard_map/ppermute | solution.py:43
  195.7 7.3 %collective-permute-done.33 = bf16[64,3072]{1,0:T(8,128)(2,1)S(1)} collective-permute-done((bf16[64,3072]{1,0:T(8,128)(2,1)S(1)}, bf16[64,3072]{1,0:T(8,128)(2,1)S(1)}, u32[]{:S(2)}, u32[]{:S(2)}) %collective-permute-start.33) | collective-permute-done | bytes 393248 | tf_op jit(solution)/shard_map/ppermute | solution.py:43
  203.0 1.6 collective-permute-done.31
  204.6 0.5 add_convert_fusion.2
  205.1 0.9 maximum_bitcast_fusion
  206.1 6.2 %all-to-all-start.2 = ((bf16[8,8,6144]{2,1,0:T(8,128)(2,1)}), bf16[8,8,6144]{2,1,0:T(8,128)(2,1)S(1)}, u32[]{:S(2)}, u32[]{:S(2)}) async-start(bf16[8,8,6144]{2,1,0:T(8,128)(2,1)} %maximum_bitcast_fusion), calls=%async_computation.2 | async-start | bytes 1572864 | tf_op jit(solution)/shard_map/all_to_all | solution.py:572
  212.3 2.8 %collective-permute-start.14 = (bf16[16,3072]{1,0:T(8,128)(2,1)S(1)}, bf16[16,3072]{1,0:T(8,128)(2,1)S(1)}, u32[]{:S(2)}, u32[]{:S(2)}) collective-permute-start(bf16[16,3072]{1,0:T(8,128)(2,1)S(1)} %get-tuple-element.94), channel_id=1, source_target_pairs={{0,64},{1,65},{2,66},{3,67},{4,68},{5,69},{6,70},{7,71},{8,72},{9,... | collective-permute-start | bytes 294920 | tf_op jit(solution)/shard_map/ppermute | solution.py:35
  215.1 6.7 %all-to-all-done.2 = bf16[8,8,6144]{2,1,0:T(8,128)(2,1)S(1)} async-done(((bf16[8,8,6144]{2,1,0:T(8,128)(2,1)}), bf16[8,8,6144]{2,1,0:T(8,128)(2,1)S(1)}, u32[]{:S(2)}, u32[]{:S(2)}) %all-to-all-start.2) | async-done | bytes 786464 | tf_op jit(solution)/shard_map/all_to_all | solution.py:572
  222.1 1.0 add_convert_fusion.7
  (96 shorter events, 3.5 us)
Async XLA Ops:
  0.0 0.8 copy-start.2
  0.8 0.8 copy-start.3
  1.5 0.7 copy-start.4
  2.2 0.7 copy-start.5
  3.2 8.6 %collective-permute-start = (bf16[144,256]{1,0:T(8,128)(2,1)S(1)}, bf16[144,256]{1,0:T(8,128)(2,1)S(1)}, u32[]{:S(2)}, u32[]{:S(2)}) collective-permute-start(bf16[144,256]{1,0:T(8,128)(2,1)S(1)} %shard_map.127), channel_id=1, source_target_pairs={{0,48},{1,49},{2,50},{3,51},{4,52},{5,53},{6,54},{7,55},{8,56},{9,... | collective-permute-start | bytes 221192 | tf_op jit(solution)/shard_map/ppermute | solution.py:43
  6.4 6.8 %collective-permute-start.1 = (bf16[144,256]{1,0:T(8,128)(2,1)S(1)}, bf16[144,256]{1,0:T(8,128)(2,1)S(1)}, u32[]{:S(2)}, u32[]{:S(2)}) collective-permute-start(bf16[144,256]{1,0:T(8,128)(2,1)S(1)} %shard_map.127), channel_id=1, source_target_pairs={{0,16},{1,17},{2,18},{3,19},{4,20},{5,21},{6,22},{7,23},{8,24},{9,... | collective-permute-start | bytes 221192 | tf_op jit(solution)/shard_map/ppermute | solution.py:43
  6.4 6.8 %collective-permute-start.2 = (bf16[144,256]{1,0:T(8,128)(2,1)S(1)}, bf16[144,256]{1,0:T(8,128)(2,1)S(1)}, u32[]{:S(2)}, u32[]{:S(2)}) collective-permute-start(bf16[144,256]{1,0:T(8,128)(2,1)S(1)} %shard_map.127), channel_id=1, source_target_pairs={{0,32},{1,33},{2,34},{3,35},{4,36},{5,37},{6,38},{7,39},{8,40},{9,... | collective-permute-start | bytes 221192 | tf_op jit(solution)/shard_map/ppermute | solution.py:43
  8.6 15.9 %collective-permute-start.4 = (bf16[768,384]{1,0:T(8,128)(2,1)}, bf16[768,384]{1,0:T(8,128)(2,1)S(1)}, u32[]{:S(2)}, u32[]{:S(2)}) collective-permute-start(bf16[768,384]{1,0:T(8,128)(2,1)} %param.19), channel_id=1, source_target_pairs={{0,48},{1,49},{2,50},{3,51},{4,52},{5,53},{6,54},{7,55},{8,56},{9,... | collective-permute-start | bytes 1769480 | tf_op jit(solution)/shard_map/ppermute | solution.py:43
  9.6 15.9 %collective-permute-start.5 = (bf16[768,384]{1,0:T(8,128)(2,1)}, bf16[768,384]{1,0:T(8,128)(2,1)S(1)}, u32[]{:S(2)}, u32[]{:S(2)}) collective-permute-start(bf16[768,384]{1,0:T(8,128)(2,1)} %param.19), channel_id=1, source_target_pairs={{0,16},{1,17},{2,18},{3,19},{4,20},{5,21},{6,22},{7,23},{8,24},{9,... | collective-permute-start | bytes 1769480 | tf_op jit(solution)/shard_map/ppermute | solution.py:43
  13.2 8.7 %collective-permute-start.3 = (bf16[4,144,256]{2,1,0:T(8,128)(2,1)S(1)}, bf16[4,144,256]{2,1,0:T(8,128)(2,1)S(1)}, u32[]{:S(2)}, u32[]{:S(2)}) collective-permute-start(bf16[4,144,256]{2,1,0:T(8,128)(2,1)S(1)} %pad_maximum_fusion), channel_id=1, source_target_pairs={{0,64},{1,65},{2,66},{3,67},{4,68},{5,69},{6,70},{7,71},{8,72},{9,... | collective-permute-start | bytes 884744 | tf_op jit(solution)/shard_map/ppermute | solution.py:35
  16.3 10.1 %copy-start.12 = (s32[16,2]{0,1:T(2,128)S(1)}, s32[16,2]{0,1:T(2,128)}, u32[]{:S(2)}) copy-start(s32[16,2]{0,1:T(2,128)} %param.24) | copy-start | bytes 388
  21.9 9.0 %copy-start.6 = (bf16[128,768]{1,0:T(8,128)(2,1)S(1)}, bf16[128,768]{1,0:T(8,128)(2,1)}, u32[]{:S(2)}) copy-start(bf16[128,768]{1,0:T(8,128)(2,1)} %queries.1) | copy-start | bytes 589828
  24.5 1.2 copy-start.7
  25.6 0.8 copy-start.8
  25.8 18.6 %collective-permute-start.7 = (bf16[768,1152]{1,0:T(8,128)(2,1)S(1)}, bf16[768,1152]{1,0:T(8,128)(2,1)}, u32[]{:S(2)}, u32[]{:S(2)}) collective-permute-start(bf16[768,1152]{1,0:T(8,128)(2,1)S(1)} %constant_dynamic-update-slice_fusion.5.near), channel_id=1, source_target_pairs={{0,8},{1,9},{2,10},{3,11},{4,12},{5,13},{6,14},{7,15},{8,0},{9,1},... | collective-permute-start | bytes 5308424 | tf_op jit(solution)/shard_map/ppermute | solution.py:39
  26.4 4.5 %collective-permute-start.6 = (bf16[8,144,256]{2,1,0:T(8,128)(2,1)S(1)}, bf16[8,144,256]{2,1,0:T(8,128)(2,1)S(1)}, u32[]{:S(2)}, u32[]{:S(2)}) collective-permute-start(bf16[8,144,256]{2,1,0:T(8,128)(2,1)S(1)} %constant_dynamic-update-slice_fusion.mine), channel_id=1, source_target_pairs={{0,8},{1,9},{2,10},{3,11},{4,12},{5,13},{6,14},{7,15},{8,0},{9,1},... | collective-permute-start | bytes 1769480 | tf_op jit(solution)/shard_map/ppermute | solution.py:39
  27.7 11.5 %copy-start.9 = (bf16[16,6144]{1,0:T(8,128)(2,1)S(1)}, bf16[16,6144]{1,0:T(8,128)(2,1)}, u32[]{:S(2)}) copy-start(bf16[16,6144]{1,0:T(8,128)(2,1)} %param.18) | copy-start | bytes 589828
  28.7 10.5 %collective-permute-start.10 = (bf16[384,384]{1,0:T(8,128)(2,1)S(1)}, bf16[384,384]{1,0:T(8,128)(2,1)S(1)}, u32[]{:S(2)}, u32[]{:S(2)}) collective-permute-start(bf16[384,384]{1,0:T(8,128)(2,1)S(1)} %slice.55), channel_id=1, source_target_pairs={{0,48},{1,49},{2,50},{3,51},{4,52},{5,53},{6,54},{7,55},{8,56},{9,... | collective-permute-start | bytes 884744 | tf_op jit(solution)/shard_map/ppermute | solution.py:43
  30.9 10.0 %collective-permute-start.9 = (bf16[384,384]{1,0:T(8,128)(2,1)S(1)}, bf16[384,384]{1,0:T(8,128)(2,1)S(1)}, u32[]{:S(2)}, u32[]{:S(2)}) collective-permute-start(bf16[384,384]{1,0:T(8,128)(2,1)S(1)} %slice.54), channel_id=1, source_target_pairs={{0,16},{1,17},{2,18},{3,19},{4,20},{5,21},{6,22},{7,23},{8,24},{9,... | collective-permute-start | bytes 884744 | tf_op jit(solution)/shard_map/ppermute | solution.py:43
  36.1 8.3 %collective-permute-start.8 = (bf16[128,768]{1,0:T(8,128)(2,1)S(1)}, bf16[128,768]{1,0:T(8,128)(2,1)S(1)}, u32[]{:S(2)}, u32[]{:S(2)}) collective-permute-start(bf16[128,768]{1,0:T(8,128)(2,1)S(1)} %shard_map.128.block), channel_id=1, source_target_pairs={{0,64},{1,65},{2,66},{3,67},{4,68},{5,69},{6,70},{7,71},{8,72},{9,... | collective-permute-start | bytes 589832 | tf_op jit(solution)/shard_map/ppermute | solution.py:35
  44.5 2.1 collective-permute-start.11
  46.6 37.6 %collective-permute-start.15 = (bf16[6144,512]{1,0:T(8,128)(2,1)}, bf16[6144,512]{1,0:T(8,128)(2,1)}, u32[]{:S(2)}, u32[]{:S(2)}) collective-permute-start(bf16[6144,512]{1,0:T(8,128)(2,1)} %bitcast.56), channel_id=1, source_target_pairs={{0,8},{1,9},{2,10},{3,11},{4,12},{5,13},{6,14},{7,15},{8,0},{9,1},... | collective-permute-start | bytes 18874376 | tf_op jit(solution)/shard_map/ppermute | solution.py:39
  46.7 37.5 %collective-permute-start.16 = (bf16[6144,512]{1,0:T(8,128)(2,1)}, bf16[6144,512]{1,0:T(8,128)(2,1)}, u32[]{:S(2)}, u32[]{:S(2)}) collective-permute-start(bf16[6144,512]{1,0:T(8,128)(2,1)} %bitcast.70), channel_id=1, source_target_pairs={{0,8},{1,9},{2,10},{3,11},{4,12},{5,13},{6,14},{7,15},{8,0},{9,1},... | collective-permute-start | bytes 18874376 | tf_op jit(solution)/shard_map/ppermute | solution.py:39
  47.1 100.2 %collective-permute-start.25 = (bf16[512,6144]{1,0:T(8,128)(2,1)}, bf16[512,6144]{1,0:T(8,128)(2,1)}, u32[]{:S(2)}, u32[]{:S(2)}) collective-permute-start(bf16[512,6144]{1,0:T(8,128)(2,1)} %bitcast.59), channel_id=1, source_target_pairs={{0,8},{1,9},{2,10},{3,11},{4,12},{5,13},{6,14},{7,15},{8,0},{9,1},... | collective-permute-start | bytes 18874376 | tf_op jit(solution)/shard_map/ppermute | solution.py:39
  53.9 29.2 %all-to-all-start = ((bf16[8,32,3072]{2,1,0:T(8,128)(2,1)}), bf16[8,32,3072]{2,1,0:T(8,128)(2,1)S(1)}, u32[]{:S(2)}, u32[]{:S(2)}) async-start(bf16[8,32,3072]{2,1,0:T(8,128)(2,1)} %shard_map.129), calls=%async_computation | async-start | bytes 3145728 | tf_op jit(solution)/shard_map/all_to_all | solution.py:502
  60.5 20.9 %collective-permute-start.13 = (s32[32]{0:T(128)S(1)}, s32[32]{0:T(128)S(1)}, u32[]{:S(2)}, u32[]{:S(2)}) collective-permute-start(s32[32]{0:T(128)S(1)} %reshape.31), channel_id=1, source_target_pairs={{0,64},{1,65},{2,66},{3,67},{4,68},{5,69},{6,70},{7,71},{8,72},{9,... | collective-permute-start | bytes 392 | tf_op jit(solution)/shard_map/ppermute | solution.py:35
  63.3 19.7 %collective-permute-start.12 = (bf16[16,3072]{1,0:T(8,128)(2,1)S(1)}, bf16[16,3072]{1,0:T(8,128)(2,1)S(1)}, u32[]{:S(2)}, u32[]{:S(2)}) collective-permute-start(bf16[16,3072]{1,0:T(8,128)(2,1)S(1)} %get-tuple-element.57), channel_id=1, source_target_pairs={{0,64},{1,65},{2,66},{3,67},{4,68},{5,69},{6,70},{7,71},{8,72},{9,... | collective-permute-start | bytes 294920 | tf_op jit(solution)/shard_map/ppermute | solution.py:35
  101.1 33.6 %copy-start.10 = (bf16[6144]{0:T(1024)(128)(2,1)S(1)}, bf16[6144]{0:T(1024)(128)(2,1)}, u32[]{:S(2)}) copy-start(bf16[6144]{0:T(1024)(128)(2,1)} %param.20) | copy-start | bytes 36868
  101.1 33.6 %dynamic-slice-start = ((bf16[6144]{0:T(1024)(128)(2,1)}, s32[]{:T(128)}), bf16[3072]{0:T(1024)(128)(2,1)S(1)}, s32[]{:S(2)}) async-start(bf16[6144]{0:T(1024)(128)(2,1)} %param.20, s32[]{:T(128)} %select_n.82), calls=%async_computation.3 | async-start | bytes 12800 | tf_op jit(solution)/shard_map/dynamic-slice
  101.1 18.1 %collective-permute-start.20 = (bf16[128,3072]{1,0:T(8,128)(2,1)S(1)}, bf16[128,3072]{1,0:T(8,128)(2,1)S(1)}, u32[]{:S(2)}, u32[]{:S(2)}) collective-permute-start(bf16[128,3072]{1,0:T(8,128)(2,1)S(1)} %bitcast.62), channel_id=1, source_target_pairs={{0,16},{1,17},{2,18},{3,19},{4,20},{5,21},{6,22},{7,23},{8,24},{9,... | collective-permute-start | bytes 2359304 | tf_op jit(solution)/shard_map/ppermute | solution.py:43
  101.4 17.9 %collective-permute-start.22 = (bf16[128,3072]{1,0:T(8,128)(2,1)S(1)}, bf16[128,3072]{1,0:T(8,128)(2,1)S(1)}, u32[]{:S(2)}, u32[]{:S(2)}) collective-permute-start(bf16[128,3072]{1,0:T(8,128)(2,1)S(1)} %bitcast.63), channel_id=1, source_target_pairs={{0,48},{1,49},{2,50},{3,51},{4,52},{5,53},{6,54},{7,55},{8,56},{9,... | collective-permute-start | bytes 2359304 | tf_op jit(solution)/shard_map/ppermute | solution.py:43
  104.3 18.3 %collective-permute-start.17 = (bf16[128,3072]{1,0:T(8,128)(2,1)S(1)}, bf16[128,3072]{1,0:T(8,128)(2,1)S(1)}, u32[]{:S(2)}, u32[]{:S(2)}) collective-permute-start(bf16[128,3072]{1,0:T(8,128)(2,1)S(1)} %bitcast.64), channel_id=1, source_target_pairs={{0,64},{1,65},{2,66},{3,67},{4,68},{5,69},{6,70},{7,71},{8,72},{9,... | collective-permute-start | bytes 2359304 | tf_op jit(solution)/shard_map/ppermute | solution.py:35
  119.2 13.3 %collective-permute-start.21 = (bf16[64,3072]{1,0:T(8,128)(2,1)S(1)}, bf16[64,3072]{1,0:T(8,128)(2,1)S(1)}, u32[]{:S(2)}, u32[]{:S(2)}) collective-permute-start(bf16[64,3072]{1,0:T(8,128)(2,1)S(1)} %slice.72), channel_id=1, source_target_pairs={{0,16},{1,17},{2,18},{3,19},{4,20},{5,21},{6,22},{7,23},{8,24},{9,... | collective-permute-start | bytes 1179656 | tf_op jit(solution)/shard_map/ppermute | solution.py:43
  119.3 13.2 %collective-permute-start.23 = (bf16[64,3072]{1,0:T(8,128)(2,1)S(1)}, bf16[64,3072]{1,0:T(8,128)(2,1)S(1)}, u32[]{:S(2)}, u32[]{:S(2)}) collective-permute-start(bf16[64,3072]{1,0:T(8,128)(2,1)S(1)} %slice.73), channel_id=1, source_target_pairs={{0,48},{1,49},{2,50},{3,51},{4,52},{5,53},{6,54},{7,55},{8,56},{9,... | collective-permute-start | bytes 1179656 | tf_op jit(solution)/shard_map/ppermute | solution.py:43
  122.6 24.7 %collective-permute-start.18 = (bf16[128,3072]{1,0:T(8,128)(2,1)S(1)}, bf16[128,3072]{1,0:T(8,128)(2,1)S(1)}, u32[]{:S(2)}, u32[]{:S(2)}) collective-permute-start(bf16[128,3072]{1,0:T(8,128)(2,1)S(1)} %collective-permute-done.17.near), channel_id=1, source_target_pairs={{0,48},{1,49},{2,50},{3,51},{4,52},{5,53},{6,54},{7,55},{8,56},{9,... | collective-permute-start | bytes 2359304 | tf_op jit(solution)/shard_map/ppermute | solution.py:43
  123.9 23.4 %collective-permute-start.19 = (bf16[128,3072]{1,0:T(8,128)(2,1)S(1)}, bf16[128,3072]{1,0:T(8,128)(2,1)S(1)}, u32[]{:S(2)}, u32[]{:S(2)}) collective-permute-start(bf16[128,3072]{1,0:T(8,128)(2,1)S(1)} %collective-permute-done.17.near), channel_id=1, source_target_pairs={{0,16},{1,17},{2,18},{3,19},{4,20},{5,21},{6,22},{7,23},{8,24},{9,... | collective-permute-start | bytes 2359304 | tf_op jit(solution)/shard_map/ppermute | solution.py:43
  132.6 14.7 %collective-permute-start.24 = (bf16[128,3072]{1,0:T(8,128)(2,1)S(1)}, bf16[128,3072]{1,0:T(8,128)(2,1)S(1)}, u32[]{:S(2)}, u32[]{:S(2)}) collective-permute-start(bf16[128,3072]{1,0:T(8,128)(2,1)S(1)} %constant_dynamic-update-slice_fusion.10.far), channel_id=1, source_target_pairs={{0,64},{1,65},{2,66},{3,67},{4,68},{5,69},{6,70},{7,71},{8,72},{9,... | collective-permute-start | bytes 2359304 | tf_op jit(solution)/shard_map/ppermute | solution.py:35
  134.8 2.8 %copy-start = (bf16[1,6144,512]{2,1,0:T(8,128)(2,1)S(1)}, bf16[1,6144,512]{2,1,0:T(8,128)(2,1)}, u32[]{:S(2)}) copy-start(bf16[1,6144,512]{2,1,0:T(8,128)(2,1)} %param.21) | copy-start | bytes 18874372
  147.3 17.1 %copy-start.11 = (f32[16,2]{0,1:T(2,128)S(1)}, f32[16,2]{0,1:T(2,128)}, u32[]{:S(2)}) copy-start(f32[16,2]{0,1:T(2,128)} %param.25) | copy-start | bytes 388
  162.8 16.2 %collective-permute-start.29 = (bf16[64,6144]{1,0:T(8,128)(2,1)}, bf16[64,6144]{1,0:T(8,128)(2,1)}, u32[]{:S(2)}, u32[]{:S(2)}) collective-permute-start(bf16[64,6144]{1,0:T(8,128)(2,1)} %get-tuple-element.82), channel_id=1, source_target_pairs={{0,64},{1,65},{2,66},{3,67},{4,68},{5,69},{6,70},{7,71},{8,72},{9,... | collective-permute-start | bytes 2359304 | tf_op jit(solution)/shard_map/ppermute | solution.py:35
  164.4 17.9 %collective-permute-start.26 = (bf16[64,6144]{1,0:T(8,128)(2,1)S(1)}, bf16[64,6144]{1,0:T(8,128)(2,1)S(1)}, u32[]{:S(2)}, u32[]{:S(2)}) collective-permute-start(bf16[64,6144]{1,0:T(8,128)(2,1)S(1)} %get-tuple-element.75), channel_id=1, source_target_pairs={{0,16},{1,17},{2,18},{3,19},{4,20},{5,21},{6,22},{7,23},{8,24},{9,... | collective-permute-start | bytes 2359304 | tf_op jit(solution)/shard_map/ppermute | solution.py:43
  165.2 17.1 %collective-permute-start.27 = (bf16[64,6144]{1,0:T(8,128)(2,1)S(1)}, bf16[64,6144]{1,0:T(8,128)(2,1)S(1)}, u32[]{:S(2)}, u32[]{:S(2)}) collective-permute-start(bf16[64,6144]{1,0:T(8,128)(2,1)S(1)} %get-tuple-element.76), channel_id=1, source_target_pairs={{0,48},{1,49},{2,50},{3,51},{4,52},{5,53},{6,54},{7,55},{8,56},{9,... | collective-permute-start | bytes 2359304 | tf_op jit(solution)/shard_map/ppermute | solution.py:43
  168.1 2.8 %copy-start.1 = (bf16[1,512,6144]{2,1,0:T(8,128)(2,1)S(1)}, bf16[1,512,6144]{2,1,0:T(8,128)(2,1)}, u32[]{:S(2)}) copy-start(bf16[1,512,6144]{2,1,0:T(8,128)(2,1)} %param.23) | copy-start | bytes 18874372
  180.2 12.1 %collective-permute-start.32 = (bf16[64,3072]{1,0:T(8,128)(2,1)S(1)}, bf16[64,3072]{1,0:T(8,128)(2,1)S(1)}, u32[]{:S(2)}, u32[]{:S(2)}) collective-permute-start(bf16[64,3072]{1,0:T(8,128)(2,1)S(1)} %get-tuple-element.91), channel_id=1, source_target_pairs={{0,48},{1,49},{2,50},{3,51},{4,52},{5,53},{6,54},{7,55},{8,56},{9,... | collective-permute-start | bytes 1179656 | tf_op jit(solution)/shard_map/ppermute | solution.py:43
  182.0 13.4 %collective-permute-start.30 = (bf16[64,3072]{1,0:T(8,128)(2,1)S(1)}, bf16[64,3072]{1,0:T(8,128)(2,1)S(1)}, u32[]{:S(2)}, u32[]{:S(2)}) collective-permute-start(bf16[64,3072]{1,0:T(8,128)(2,1)S(1)} %get-tuple-element.92), channel_id=1, source_target_pairs={{0,16},{1,17},{2,18},{3,19},{4,20},{5,21},{6,22},{7,23},{8,24},{9,... | collective-permute-start | bytes 1179656 | tf_op jit(solution)/shard_map/ppermute | solution.py:43
  182.6 22.0 %collective-permute-start.28 = (bf16[64,6144]{1,0:T(8,128)(2,1)S(1)}, bf16[64,6144]{1,0:T(8,128)(2,1)S(1)}, u32[]{:S(2)}, u32[]{:S(2)}) collective-permute-start(bf16[64,6144]{1,0:T(8,128)(2,1)S(1)} %add_convert_fusion), channel_id=1, source_target_pairs={{0,64},{1,65},{2,66},{3,67},{4,68},{5,69},{6,70},{7,71},{8,72},{9,... | collective-permute-start | bytes 2359304 | tf_op jit(solution)/shard_map/ppermute | solution.py:35
  184.7 19.9 %collective-permute-start.34 = (bf16[64,3072]{1,0:T(8,128)(2,1)S(1)}, bf16[64,3072]{1,0:T(8,128)(2,1)S(1)}, u32[]{:S(2)}, u32[]{:S(2)}) collective-permute-start(bf16[64,3072]{1,0:T(8,128)(2,1)S(1)} %get-tuple-element.85), channel_id=1, source_target_pairs={{0,48},{1,49},{2,50},{3,51},{4,52},{5,53},{6,54},{7,55},{8,56},{9,... | collective-permute-start | bytes 1179656 | tf_op jit(solution)/shard_map/ppermute | solution.py:43
  187.7 17.0 %collective-permute-start.35 = (bf16[64,3072]{1,0:T(8,128)(2,1)S(1)}, bf16[64,3072]{1,0:T(8,128)(2,1)S(1)}, u32[]{:S(2)}, u32[]{:S(2)}) collective-permute-start(bf16[64,3072]{1,0:T(8,128)(2,1)S(1)} %get-tuple-element.87), channel_id=1, source_target_pairs={{0,16},{1,17},{2,18},{3,19},{4,20},{5,21},{6,22},{7,23},{8,24},{9,... | collective-permute-start | bytes 1179656 | tf_op jit(solution)/shard_map/ppermute | solution.py:43
  192.5 10.6 %collective-permute-start.33 = (bf16[64,3072]{1,0:T(8,128)(2,1)S(1)}, bf16[64,3072]{1,0:T(8,128)(2,1)S(1)}, u32[]{:S(2)}, u32[]{:S(2)}) collective-permute-start(bf16[64,3072]{1,0:T(8,128)(2,1)S(1)} %add_convert_fusion.3), channel_id=1, source_target_pairs={{0,48},{1,49},{2,50},{3,51},{4,52},{5,53},{6,54},{7,55},{8,56},{9,... | collective-permute-start | bytes 1179656 | tf_op jit(solution)/shard_map/ppermute | solution.py:43
  195.6 9.1 %collective-permute-start.31 = (bf16[64,3072]{1,0:T(8,128)(2,1)S(1)}, bf16[64,3072]{1,0:T(8,128)(2,1)S(1)}, u32[]{:S(2)}, u32[]{:S(2)}) collective-permute-start(bf16[64,3072]{1,0:T(8,128)(2,1)S(1)} %add_convert_fusion.5), channel_id=1, source_target_pairs={{0,16},{1,17},{2,18},{3,19},{4,20},{5,21},{6,22},{7,23},{8,24},{9,... | collective-permute-start | bytes 1179656 | tf_op jit(solution)/shard_map/ppermute | solution.py:43
  206.1 15.7 %all-to-all-start.2 = ((bf16[8,8,6144]{2,1,0:T(8,128)(2,1)}), bf16[8,8,6144]{2,1,0:T(8,128)(2,1)S(1)}, u32[]{:S(2)}, u32[]{:S(2)}) async-start(bf16[8,8,6144]{2,1,0:T(8,128)(2,1)} %maximum_bitcast_fusion), calls=%async_computation.2 | async-start | bytes 1572864 | tf_op jit(solution)/shard_map/all_to_all | solution.py:572
  212.3 9.7 %collective-permute-start.14 = (bf16[16,3072]{1,0:T(8,128)(2,1)S(1)}, bf16[16,3072]{1,0:T(8,128)(2,1)S(1)}, u32[]{:S(2)}, u32[]{:S(2)}) collective-permute-start(bf16[16,3072]{1,0:T(8,128)(2,1)S(1)} %get-tuple-element.94), channel_id=1, source_target_pairs={{0,64},{1,65},{2,66},{3,67},{4,68},{5,69},{6,70},{7,71},{8,72},{9,... | collective-permute-start | bytes 294920 | tf_op jit(solution)/shard_map/ppermute | solution.py:35
where the time goes:
time: 224 us; the launch traced here: 223 us
  waiting for transfers between devices  77.3 us (35%)
  starting transfers between devices  63.6 us (28%)
  Pallas kernels  46.4 us (21%)
  blocking collectives  16.9 us (8%)
  local copies, waits for them, and re-layouts  13.2 us (6%)
  other arithmetic  3.89 us (2%)
    ppermute x21, waiting for transfers between devices, from_y(): return lax.ppermute(value, BOTH, partner(step_y=-step))  41.1 us
    ppermute x21, starting transfers between devices, from_y(): return lax.ppermute(value, BOTH, partner(step_y=-step))  30 us
    ppermute x9, waiting for transfers between devices, flip_x(): return lax.ppermute(value, BOTH, partner(flip_x=1))  27.5 us
    ppermute x9, starting transfers between devices, flip_x(): return lax.ppermute(value, BOTH, partner(flip_x=1))  20.3 us
    all_to_all x1, blocking collectives, per_device(): lax.all_to_all(outgoing.reshape(NE, 2 * CAP, half), 'exp', split_axis=0,...  16.9 us
    pallas_call x1, Pallas kernels, expert_rest(): pl.pallas_call(finish, out_shape=[jax.ShapeDtypeStruct((2, NY, rows // 2,...  15.4 us
    unnamed x35, local copies, waits for them, and re-layouts  10.4 us
    pallas_call x1, Pallas kernels, expert_in(): pl.pallas_call(begin, grid_spec=pltpu.PrefetchScalarGridSpec(num_scalar_p...  9.66 us
  transfers between devices with their start and end apart: 38, of which 15 were waited for; matrix products, arithmetic and copies ran while one was open for 3% of the time, Pallas kernels for 14%

commit v1 on v0

--- a/solution.py
+++ b/solution.py
@@ -157,7 +157,7 @@
         in_specs=[pl.BlockSpec(memory_space=pltpu.SMEM), vmem, vmem, vmem],
         out_specs=vmem,
         scratch_shapes=[pltpu.VMEM((queries.size // HD, 16 * tok), F32)],
-        compiler_params=pltpu.CompilerParams(vmem_limit_bytes=24 * 2**20),
+        compiler_params=pltpu.CompilerParams(vmem_limit_bytes=40 * 2**20),
         cost_estimate=pl.CostEstimate(
             flops=4 * queries.size * 16 * tok, bytes_accessed=1600000, transcendentals=1600000
         ),
@@ -165,42 +165,28 @@
 
 
 def project(block, across, near, far, near_other, far_other, out):
-    step, half = pl.program_id(0), pl.num_programs(0) // 2
     rows = out.shape[1] // 2
     both = jnp.concatenate(
         [block[...].reshape(NE, 1, rows, -1), across[...].reshape(NE, 1, rows, -1)], 1
     ).reshape(NE * 2 * rows, -1)
-
-    def store(weight):
-        product = jnp.dot(both, weight[...], preferred_element_type=F32)
-        out[...] = product.astype(BF16).reshape(out.shape)
-
-    pl.when(step < half - 1)(lambda: store(near))
-    pl.when(step == half - 1)(lambda: store(far))
-    pl.when((step >= half) & (step < 2 * half - 1))(lambda: store(near_other))
-    pl.when(step == 2 * half - 1)(lambda: store(far_other))
+    part = far.shape[1]
+    weights = [(ref, i) for ref in (near, far, near_other, far_other) for i in range(ref.shape[1] // part)]
+    for n, (ref, i) in enumerate(weights):
+        product = jnp.dot(both, ref[:, i * part : (i + 1) * part], preferred_element_type=F32)
+        out[:, :, n * part : (n + 1) * part] = product.astype(BF16).reshape(NE, 2 * rows, part)
 
 
 def projection(block, across, near, far, near_other, far_other, rows):
-    depth, part = far.shape
-    whole = pl.BlockSpec(block.shape, lambda i: (0, 0))
-    single = pl.BlockSpec((depth, part), lambda i: (0, 0))
+    vmem = pl.BlockSpec(memory_space=pltpu.VMEM)
+    columns = 2 * (near.shape[1] + far.shape[1])
     return pl.pallas_call(
         project,
-        grid=(2 * NY,),
-        out_shape=jax.ShapeDtypeStruct((NE, 2 * rows, 2 * NY * part), BF16),
-        in_specs=[
-            whole,
-            whole,
-            pl.BlockSpec((depth, part), lambda i: (0, jnp.minimum(i, NY - 2))),
-            single,
-            pl.BlockSpec((depth, part), lambda i: (0, jnp.clip(i - NY, 0, NY - 2))),
-            single,
-        ],
-        out_specs=pl.BlockSpec((NE, 2 * rows, part), lambda i: (0, 0, i)),
+        out_shape=jax.ShapeDtypeStruct((NE, 2 * rows, columns), BF16),
+        in_specs=[vmem] * 6,
+        out_specs=vmem,
         compiler_params=pltpu.CompilerParams(vmem_limit_bytes=24 * 2**20),
         cost_estimate=pl.CostEstimate(
-            flops=16 * block.size * NY * part, bytes_accessed=6500000, transcendentals=0
+            flops=4 * block.size * columns, bytes_accessed=6500000, transcendentals=0
         ),
     )(block, across, near, far, near_other, far_other)
 

time: 224 us -> 222 us (level)
  local copies, waits for them, and re-layouts: 13.2 us -> 18 us
  waiting for transfers between devices: 77.3 us -> 73.6 us
  Pallas kernels: 46.4 us -> 43.4 us
    pallas_call x1, Pallas kernels: 6.65 us -> 2.95 us  [projection(): pl.pallas_call(project, out_shape=jax.ShapeDtypeStruct((NE, 2 * rows, col...]
    unnamed x35 -> x39, local copies, waits for them, and re-layouts: 10.4 us -> 13.8 us
    ppermute x21, waiting for transfers between devices: 41.1 us -> 38.1 us  [from_y(): return lax.ppermute(value, BOTH, partner(step_y=-step))]
  transfers between devices with their start and end apart: 38 -> 38, of which waited for: 15 -> 14; matrix products, arithmetic and copies ran while one was open for 3% -> 5% of each run, Pallas kernels for 14% -> 12%
where the time goes in v1:
time: 222 us; the launch traced here: 221 us
  waiting for transfers between devices  73.6 us (33%)
  starting transfers between devices  63.4 us (29%)
  Pallas kernels  43.4 us (20%)
  local copies, waits for them, and re-layouts  18 us (8%)
  blocking collectives  16.9 us (8%)
  other arithmetic  3.9 us (2%)
    ppermute x21, waiting for transfers between devices, from_y(): return lax.ppermute(value, BOTH, partner(step_y=-step))  38.1 us
    ppermute x21, starting transfers between devices, from_y(): return lax.ppermute(value, BOTH, partner(step_y=-step))  29.9 us
    ppermute x9, waiting for transfers between devices, flip_x(): return lax.ppermute(value, BOTH, partner(flip_x=1))  26.8 us
    ppermute x9, starting transfers between devices, flip_x(): return lax.ppermute(value, BOTH, partner(flip_x=1))  20.6 us
    all_to_all x1, blocking collectives, per_device(): lax.all_to_all(outgoing.reshape(NE, 2 * CAP, half), 'exp', split_axis=0,...  16.9 us
    pallas_call x1, Pallas kernels, expert_rest(): pl.pallas_call(finish, out_shape=[jax.ShapeDtypeStruct((2, NY, rows // 2,...  15.4 us
    unnamed x39, local copies, waits for them, and re-layouts  13.8 us
    pallas_call x1, Pallas kernels, expert_in(): pl.pallas_call(begin, grid_spec=pltpu.PrefetchScalarGridSpec(num_scalar_p...  9.67 us
  transfers between devices with their start and end apart: 38, of which 14 were waited for; matrix products, arithmetic and copies ran while one was open for 5% of the time, Pallas kernels for 12%

profile of v1, /device:TPU:0, one launch (start us, length us, event | category | flops | bytes accessed | tf_op | source)
XLA Modules:
  0.0 220.9 jit_solution(17664053246015716914)
XLA Ops:
  0.0 0.8 copy-done.3
  0.8 0.8 copy-done.4
  1.5 0.7 copy-done.5
  2.2 0.7 copy-done.6
  3.2 3.2 %collective-permute-start = (bf16[144,256]{1,0:T(8,128)(2,1)S(1)}, bf16[144,256]{1,0:T(8,128)(2,1)S(1)}, u32[]{:S(2)}, u32[]{:S(2)}) collective-permute-start(bf16[144,256]{1,0:T(8,128)(2,1)S(1)} %shard_map.127), channel_id=1, source_target_pairs={{0,48},{1,49},{2,50},{3,51},{4,52},{5,53},{6,54},{7,55},{8,56},{9,... | collective-permute-start | bytes 221192 | tf_op jit(solution)/shard_map/ppermute | solution.py:43
  6.4 2.2 collective-permute-start.2
  8.6 1.1 collective-permute-start.4
  9.6 1.0 collective-permute-start.5
  10.6 0.6 constant_dynamic-update-slice_fusion.4
  11.2 1.1 constant_dynamic-update-slice_fusion.7
  12.4 0.8 collective-permute-done.1
  13.2 3.1 %collective-permute-start.3 = (bf16[4,144,256]{2,1,0:T(8,128)(2,1)S(1)}, bf16[4,144,256]{2,1,0:T(8,128)(2,1)S(1)}, u32[]{:S(2)}, u32[]{:S(2)}) collective-permute-start(bf16[4,144,256]{2,1,0:T(8,128)(2,1)S(1)} %pad_maximum_fusion), channel_id=1, source_target_pairs={{0,64},{1,65},{2,66},{3,67},{4,68},{5,69},{6,70},{7,71},{8,72},{9,... | collective-permute-start | bytes 884744 | tf_op jit(solution)/shard_map/ppermute | solution.py:35
  16.3 0.6 constant_dynamic-update-slice_fusion.3
  17.5 0.6 constant_dynamic-update-slice_fusion.1
  18.2 3.7 %collective-permute-done.3 = bf16[4,144,256]{2,1,0:T(8,128)(2,1)S(1)} collective-permute-done((bf16[4,144,256]{2,1,0:T(8,128)(2,1)S(1)}, bf16[4,144,256]{2,1,0:T(8,128)(2,1)S(1)}, u32[]{:S(2)}, u32[]{:S(2)}) %collective-permute-start.3) | collective-permute-done | bytes 294944 | tf_op jit(solution)/shard_map/ppermute | solution.py:35
  21.9 0.7 constant_dynamic-update-slice_fusion.mine
  22.6 1.9 collective-permute-done.4
  24.5 1.0 collective-permute-done.5
  26.7 1.0 slice.55
  27.7 1.0 slice.54
  28.7 2.1 collective-permute-start.10
  30.9 0.9 copy-done.7
  31.8 5.8 %shard_map.128.block = bf16[128,768]{1,0:T(8,128)(2,1)S(1)} custom-call(s32[16]{0:T(128)S(1)} %stack.103.start, bf16[128,768]{1,0:T(8,128)(2,1)S(1)} %copy-done.7, bf16[8,144,256]{2,1,0:T(8,128)(2,1)} %constant_dynamic-update-slice_fusion.mine, bf16[8,144,256]{2,1,0:T(8,128)(2,1)} %collective-permute-done.6.other), custom_call_target="tpu_custom_call" | custom-call | flops 805306368 | bytes 1600000 | tf_op jit(solution)/shard_map/pallas_call | solution.py:154
  37.6 3.1 %collective-permute-start.8 = (bf16[128,768]{1,0:T(8,128)(2,1)S(1)}, bf16[128,768]{1,0:T(8,128)(2,1)S(1)}, u32[]{:S(2)}, u32[]{:S(2)}) collective-permute-start(bf16[128,768]{1,0:T(8,128)(2,1)S(1)} %shard_map.128.block), channel_id=1, source_target_pairs={{0,64},{1,65},{2,66},{3,67},{4,68},{5,69},{6,70},{7,71},{8,72},{9,... | collective-permute-start | bytes 589832 | tf_op jit(solution)/shard_map/ppermute | solution.py:35
  40.7 0.7 constant_dynamic-slice_fusion
  41.4 4.6 %collective-permute-done.8.across = bf16[128,768]{1,0:T(8,128)(2,1)S(1)} collective-permute-done((bf16[128,768]{1,0:T(8,128)(2,1)S(1)}, bf16[128,768]{1,0:T(8,128)(2,1)S(1)}, u32[]{:S(2)}, u32[]{:S(2)}) %collective-permute-start.8) | collective-permute-done | bytes 196640 | tf_op jit(solution)/shard_map/ppermute | solution.py:35
  46.2 2.0 collective-permute-done.11.far_other
  48.8 2.9 %shard_map.129 = bf16[8,32,3072]{2,1,0:T(8,128)(2,1)} custom-call(bf16[128,768]{1,0:T(8,128)(2,1)S(1)} %shard_map.128.block, bf16[128,768]{1,0:T(8,128)(2,1)S(1)} %collective-permute-done.8.across, bf16[768,1152]{1,0:T(8,128)(2,1)S(1)} %constant_dynamic-update-slice_fusion.5.near, bf16[768,384]{1,0:T(8,128)(2,1)S(1)} %constant_dynamic-update-slice_fusion.8.far, ...), custom_call_target="tpu_custom_call" | custom-call | flops 1207959552 | bytes 6500000 | tf_op jit(solution)/shard_map/pallas_call | solution.py:182
  51.8 6.4 %all-to-all-start = ((bf16[8,32,3072]{2,1,0:T(8,128)(2,1)}), bf16[8,32,3072]{2,1,0:T(8,128)(2,1)S(1)}, u32[]{:S(2)}, u32[]{:S(2)}) async-start(bf16[8,32,3072]{2,1,0:T(8,128)(2,1)} %shard_map.129), calls=%async_computation | async-start | bytes 3145728 | tf_op jit(solution)/shard_map/all_to_all | solution.py:488
  58.6 2.8 %collective-permute-start.13 = (s32[32]{0:T(128)S(1)}, s32[32]{0:T(128)S(1)}, u32[]{:S(2)}, u32[]{:S(2)}) collective-permute-start(s32[32]{0:T(128)S(1)} %reshape.31), channel_id=1, source_target_pairs={{0,64},{1,65},{2,66},{3,67},{4,68},{5,69},{6,70},{7,71},{8,72},{9,... | collective-permute-start | bytes 392 | tf_op jit(solution)/shard_map/ppermute | solution.py:35
  61.3 0.8 collective-permute-start.12
  62.1 17.3 %collective-permute-done.13 = s32[32]{0:T(128)S(1)} collective-permute-done((s32[32]{0:T(128)S(1)}, s32[32]{0:T(128)S(1)}, u32[]{:S(2)}, u32[]{:S(2)}) %collective-permute-start.13) | collective-permute-done | bytes 160 | tf_op jit(solution)/shard_map/ppermute | solution.py:35
  79.9 1.1 collective-permute-done.12.res_across
  81.1 1.1 shard_map.130
  82.2 16.9 %all_to_all.15 = bf16[8,16,3072]{2,1,0:T(8,128)(2,1)S(1)} all-to-all(bf16[8,16,3072]{2,1,0:T(8,128)(2,1)S(1)} %bitcast.66), channel_id=1, replica_groups=mesh['ctx'=16,'exp'=8] {'exp'}, dimensions={0} | all-to-all | bytes 1572864 | tf_op jit(solution)/shard_map/all_to_all | solution.py:502
  99.7 2.7 %collective-permute-start.22 = (bf16[128,3072]{1,0:T(8,128)(2,1)S(1)}, bf16[128,3072]{1,0:T(8,128)(2,1)S(1)}, u32[]{:S(2)}, u32[]{:S(2)}) collective-permute-start(bf16[128,3072]{1,0:T(8,128)(2,1)S(1)} %bitcast.63), channel_id=1, source_target_pairs={{0,48},{1,49},{2,50},{3,51},{4,52},{5,53},{6,54},{7,55},{8,56},{9,... | collective-permute-start | bytes 2359304 | tf_op jit(solution)/shard_map/ppermute | solution.py:43
  102.3 2.0 collective-permute-start.17
  104.4 12.8 %collective-permute-done.20.below = bf16[128,3072]{1,0:T(8,128)(2,1)S(1)} collective-permute-done((bf16[128,3072]{1,0:T(8,128)(2,1)S(1)}, bf16[128,3072]{1,0:T(8,128)(2,1)S(1)}, u32[]{:S(2)}, u32[]{:S(2)}) %collective-permute-start.20) | collective-permute-done | bytes 786464 | tf_op jit(solution)/shard_map/ppermute | solution.py:43
  117.3 3.3 %collective-permute-start.23 = (bf16[64,3072]{1,0:T(8,128)(2,1)S(1)}, bf16[64,3072]{1,0:T(8,128)(2,1)S(1)}, u32[]{:S(2)}, u32[]{:S(2)}) collective-permute-start(bf16[64,3072]{1,0:T(8,128)(2,1)S(1)} %slice.73), channel_id=1, source_target_pairs={{0,48},{1,49},{2,50},{3,51},{4,52},{5,53},{6,54},{7,55},{8,56},{9,... | collective-permute-start | bytes 1179656 | tf_op jit(solution)/shard_map/ppermute | solution.py:43
  120.6 1.2 collective-permute-start.18
  121.8 0.8 collective-permute-start.19
  122.6 7.9 %collective-permute-done.21 = bf16[64,3072]{1,0:T(8,128)(2,1)S(1)} collective-permute-done((bf16[64,3072]{1,0:T(8,128)(2,1)S(1)}, bf16[64,3072]{1,0:T(8,128)(2,1)S(1)}, u32[]{:S(2)}, u32[]{:S(2)}) %collective-permute-start.21) | collective-permute-done | bytes 393248 | tf_op jit(solution)/shard_map/ppermute | solution.py:43
  130.6 2.3 %collective-permute-start.24 = (bf16[128,3072]{1,0:T(8,128)(2,1)S(1)}, bf16[128,3072]{1,0:T(8,128)(2,1)S(1)}, u32[]{:S(2)}, u32[]{:S(2)}) collective-permute-start(bf16[128,3072]{1,0:T(8,128)(2,1)S(1)} %constant_dynamic-update-slice_fusion.10.far), channel_id=1, source_target_pairs={{0,64},{1,65},{2,66},{3,67},{4,68},{5,69},{6,70},{7,71},{8,72},{9,... | collective-permute-start | bytes 2359304 | tf_op jit(solution)/shard_map/ppermute | solution.py:35
  133.0 2.8 %copy-done = bf16[1,6144,512]{2,1,0:T(8,128)(2,1)S(1)} copy-done((bf16[1,6144,512]{2,1,0:T(8,128)(2,1)S(1)}, bf16[1,6144,512]{2,1,0:T(8,128)(2,1)}, u32[]{:S(2)}) %copy-start) | copy-done | bytes 6291480
  135.8 9.7 %shard_map.131 = (f32[4,512,512]{2,1,0:T(8,128)S(1)}, f32[512,128]{1,0:T(8,128)S(1)}) custom-call(s32[1]{0:T(128)} %bitcast.32.which, bf16[128,3072]{1,0:T(8,128)(2,1)S(1)} %bitcast.65, bf16[128,3072]{1,0:T(8,128)(2,1)S(1)} %collective-permute-done.22.above, bf16[128,3072]{1,0:T(8,128)(2,1)S(1)} %collective-permute-done.20.below, ...), custom_call_target="tpu_custom_call" | custom-call | flops 6442450944 | bytes 16000000 | tf_op jit(solution)/shard_map/pallas_call | solution.py:359
  145.6 15.4 %shard_map.132 = (bf16[2,4,64,1024]{3,2,1,0:T(8,128)(2,1)S(1)}, bf16[64,6144]{1,0:T(8,128)(2,1)S(1)}, bf16[64,6144]{1,0:T(8,128)(2,1)S(1)}, bf16[64,6144]{1,0:T(8,128)(2,1)}) custom-call(s32[2]{0:T(128)S(1)} %pad_add_fusion.1.which, bf16[128,3072]{1,0:T(8,128)(2,1)S(1)} %collective-permute-done.17.near, bf16[128,3072]{1,0:T(8,128)(2,1)S(1)} %collective-permute-done.18.above, ...), custom_call_target="tpu_custom_call" | custom-call | flops 9663676416 | bytes 26000000 | tf_op jit(solution)/shard_map/pallas_call | solution.py:332
  161.0 1.6 collective-permute-start.29
  162.7 0.7 collective-permute-start.26
  163.4 3.0 %collective-permute-start.27 = (bf16[64,6144]{1,0:T(8,128)(2,1)S(1)}, bf16[64,6144]{1,0:T(8,128)(2,1)S(1)}, u32[]{:S(2)}, u32[]{:S(2)}) collective-permute-start(bf16[64,6144]{1,0:T(8,128)(2,1)S(1)} %get-tuple-element.76), channel_id=1, source_target_pairs={{0,48},{1,49},{2,50},{3,51},{4,52},{5,53},{6,54},{7,55},{8,56},{9,... | collective-permute-start | bytes 2359304 | tf_op jit(solution)/shard_map/ppermute | solution.py:43
  166.4 2.8 %copy-done.1 = bf16[1,512,6144]{2,1,0:T(8,128)(2,1)S(1)} copy-done((bf16[1,512,6144]{2,1,0:T(8,128)(2,1)S(1)}, bf16[1,512,6144]{2,1,0:T(8,128)(2,1)}, u32[]{:S(2)}) %copy-start.1) | copy-done | bytes 6291480
  169.1 8.1 %shard_map.133 = (bf16[64,3072]{1,0:T(8,128)(2,1)S(1)}, bf16[64,3072]{1,0:T(8,128)(2,1)S(1)}, bf16[64,3072]{1,0:T(8,128)(2,1)S(1)}, bf16[64,3072]{1,0:T(8,128)(2...) custom-call(bf16[2,4,64,1024]{3,2,1,0:T(8,128)(2,1)S(1)} %get-tuple-element.72.hid, ...), custom_call_target="tpu_custom_call" | custom-call | flops 4026531840 | bytes 15000000 | tf_op jit(solution)/shard_map/pallas_call | solution.py:420
  177.2 1.3 add_convert_fusion.4
  178.5 1.8 collective-permute-start.32
  180.9 2.1 collective-permute-start.28
  183.0 2.9 %collective-permute-start.34 = (bf16[64,3072]{1,0:T(8,128)(2,1)S(1)}, bf16[64,3072]{1,0:T(8,128)(2,1)S(1)}, u32[]{:S(2)}, u32[]{:S(2)}) collective-permute-start(bf16[64,3072]{1,0:T(8,128)(2,1)S(1)} %get-tuple-element.85), channel_id=1, source_target_pairs={{0,48},{1,49},{2,50},{3,51},{4,52},{5,53},{6,54},{7,55},{8,56},{9,... | collective-permute-start | bytes 1179656 | tf_op jit(solution)/shard_map/ppermute | solution.py:43
  185.9 4.7 %collective-permute-done.32 = bf16[64,3072]{1,0:T(8,128)(2,1)S(1)} collective-permute-done((bf16[64,3072]{1,0:T(8,128)(2,1)S(1)}, bf16[64,3072]{1,0:T(8,128)(2,1)S(1)}, u32[]{:S(2)}, u32[]{:S(2)}) %collective-permute-start.32) | collective-permute-done | bytes 393248 | tf_op jit(solution)/shard_map/ppermute | solution.py:43
  190.8 3.0 %collective-permute-start.33 = (bf16[64,3072]{1,0:T(8,128)(2,1)S(1)}, bf16[64,3072]{1,0:T(8,128)(2,1)S(1)}, u32[]{:S(2)}, u32[]{:S(2)}) collective-permute-start(bf16[64,3072]{1,0:T(8,128)(2,1)S(1)} %add_convert_fusion.3), channel_id=1, source_target_pairs={{0,48},{1,49},{2,50},{3,51},{4,52},{5,53},{6,54},{7,55},{8,56},{9,... | collective-permute-start | bytes 1179656 | tf_op jit(solution)/shard_map/ppermute | solution.py:43
  193.9 7.2 %collective-permute-done.33 = bf16[64,3072]{1,0:T(8,128)(2,1)S(1)} collective-permute-done((bf16[64,3072]{1,0:T(8,128)(2,1)S(1)}, bf16[64,3072]{1,0:T(8,128)(2,1)S(1)}, u32[]{:S(2)}, u32[]{:S(2)}) %collective-permute-start.33) | collective-permute-done | bytes 393248 | tf_op jit(solution)/shard_map/ppermute | solution.py:43
  201.1 1.7 collective-permute-done.31
  203.4 1.0 maximum_bitcast_fusion
  204.3 5.8 %all-to-all-start.2 = ((bf16[8,8,6144]{2,1,0:T(8,128)(2,1)}), bf16[8,8,6144]{2,1,0:T(8,128)(2,1)S(1)}, u32[]{:S(2)}, u32[]{:S(2)}) async-start(bf16[8,8,6144]{2,1,0:T(8,128)(2,1)} %maximum_bitcast_fusion), calls=%async_computation.2 | async-start | bytes 1572864 | tf_op jit(solution)/shard_map/all_to_all | solution.py:558
  210.1 2.8 %collective-permute-start.14 = (bf16[16,3072]{1,0:T(8,128)(2,1)S(1)}, bf16[16,3072]{1,0:T(8,128)(2,1)S(1)}, u32[]{:S(2)}, u32[]{:S(2)}) collective-permute-start(bf16[16,3072]{1,0:T(8,128)(2,1)S(1)} %get-tuple-element.94), channel_id=1, source_target_pairs={{0,64},{1,65},{2,66},{3,67},{4,68},{5,69},{6,70},{7,71},{8,72},{9,... | collective-permute-start | bytes 294920 | tf_op jit(solution)/shard_map/ppermute | solution.py:35
  212.9 6.7 %all-to-all-done.2 = bf16[8,8,6144]{2,1,0:T(8,128)(2,1)S(1)} async-done(((bf16[8,8,6144]{2,1,0:T(8,128)(2,1)}), bf16[8,8,6144]{2,1,0:T(8,128)(2,1)S(1)}, u32[]{:S(2)}, u32[]{:S(2)}) %all-to-all-start.2) | async-done | bytes 786464 | tf_op jit(solution)/shard_map/all_to_all | solution.py:558
  219.9 1.0 add_convert_fusion.7
  (100 shorter events, 6.5 us)
Async XLA Ops:
  0.0 0.8 copy-start.3
  0.8 0.8 copy-start.4
  1.5 0.7 copy-start.5
  2.2 0.7 copy-start.6
  3.2 9.2 %collective-permute-start = (bf16[144,256]{1,0:T(8,128)(2,1)S(1)}, bf16[144,256]{1,0:T(8,128)(2,1)S(1)}, u32[]{:S(2)}, u32[]{:S(2)}) collective-permute-start(bf16[144,256]{1,0:T(8,128)(2,1)S(1)} %shard_map.127), channel_id=1, source_target_pairs={{0,48},{1,49},{2,50},{3,51},{4,52},{5,53},{6,54},{7,55},{8,56},{9,... | collective-permute-start | bytes 221192 | tf_op jit(solution)/shard_map/ppermute | solution.py:43
  6.4 6.8 %collective-permute-start.1 = (bf16[144,256]{1,0:T(8,128)(2,1)S(1)}, bf16[144,256]{1,0:T(8,128)(2,1)S(1)}, u32[]{:S(2)}, u32[]{:S(2)}) collective-permute-start(bf16[144,256]{1,0:T(8,128)(2,1)S(1)} %shard_map.127), channel_id=1, source_target_pairs={{0,16},{1,17},{2,18},{3,19},{4,20},{5,21},{6,22},{7,23},{8,24},{9,... | collective-permute-start | bytes 221192 | tf_op jit(solution)/shard_map/ppermute | solution.py:43
  6.4 6.8 %collective-permute-start.2 = (bf16[144,256]{1,0:T(8,128)(2,1)S(1)}, bf16[144,256]{1,0:T(8,128)(2,1)S(1)}, u32[]{:S(2)}, u32[]{:S(2)}) collective-permute-start(bf16[144,256]{1,0:T(8,128)(2,1)S(1)} %shard_map.127), channel_id=1, source_target_pairs={{0,32},{1,33},{2,34},{3,35},{4,36},{5,37},{6,38},{7,39},{8,40},{9,... | collective-permute-start | bytes 221192 | tf_op jit(solution)/shard_map/ppermute | solution.py:43
  8.6 15.9 %collective-permute-start.4 = (bf16[768,384]{1,0:T(8,128)(2,1)}, bf16[768,384]{1,0:T(8,128)(2,1)S(1)}, u32[]{:S(2)}, u32[]{:S(2)}) collective-permute-start(bf16[768,384]{1,0:T(8,128)(2,1)} %param.19), channel_id=1, source_target_pairs={{0,48},{1,49},{2,50},{3,51},{4,52},{5,53},{6,54},{7,55},{8,56},{9,... | collective-permute-start | bytes 1769480 | tf_op jit(solution)/shard_map/ppermute | solution.py:43
  9.6 15.9 %collective-permute-start.5 = (bf16[768,384]{1,0:T(8,128)(2,1)}, bf16[768,384]{1,0:T(8,128)(2,1)S(1)}, u32[]{:S(2)}, u32[]{:S(2)}) collective-permute-start(bf16[768,384]{1,0:T(8,128)(2,1)} %param.19), channel_id=1, source_target_pairs={{0,16},{1,17},{2,18},{3,19},{4,20},{5,21},{6,22},{7,23},{8,24},{9,... | collective-permute-start | bytes 1769480 | tf_op jit(solution)/shard_map/ppermute | solution.py:43
  13.2 8.7 %collective-permute-start.3 = (bf16[4,144,256]{2,1,0:T(8,128)(2,1)S(1)}, bf16[4,144,256]{2,1,0:T(8,128)(2,1)S(1)}, u32[]{:S(2)}, u32[]{:S(2)}) collective-permute-start(bf16[4,144,256]{2,1,0:T(8,128)(2,1)S(1)} %pad_maximum_fusion), channel_id=1, source_target_pairs={{0,64},{1,65},{2,66},{3,67},{4,68},{5,69},{6,70},{7,71},{8,72},{9,... | collective-permute-start | bytes 884744 | tf_op jit(solution)/shard_map/ppermute | solution.py:35
  16.9 9.5 %copy-start.14 = (s32[16,2]{0,1:T(2,128)S(1)}, s32[16,2]{0,1:T(2,128)}, u32[]{:S(2)}) copy-start(s32[16,2]{0,1:T(2,128)} %param.24) | copy-start | bytes 388
  24.5 1.2 copy-start.8
  25.6 0.8 copy-start.9
  25.8 20.2 %collective-permute-start.7 = (bf16[768,1152]{1,0:T(8,128)(2,1)S(1)}, bf16[768,1152]{1,0:T(8,128)(2,1)S(1)}, u32[]{:S(2)}, u32[]{:S(2)}) collective-permute-start(bf16[768,1152]{1,0:T(8,128)(2,1)S(1)} %constant_dynamic-update-slice_fusion.5.near), channel_id=1, source_target_pairs={{0,8},{1,9},{2,10},{3,11},{4,12},{5,13},{6,14},{7,15},{8,0},{9,1},... | collective-permute-start | bytes 5308424 | tf_op jit(solution)/shard_map/ppermute | solution.py:39
  26.4 4.5 %collective-permute-start.6 = (bf16[8,144,256]{2,1,0:T(8,128)(2,1)}, bf16[8,144,256]{2,1,0:T(8,128)(2,1)}, u32[]{:S(2)}, u32[]{:S(2)}) collective-permute-start(bf16[8,144,256]{2,1,0:T(8,128)(2,1)} %constant_dynamic-update-slice_fusion.mine), channel_id=1, source_target_pairs={{0,8},{1,9},{2,10},{3,11},{4,12},{5,13},{6,14},{7,15},{8,0},{9,1},... | collective-permute-start | bytes 1769480 | tf_op jit(solution)/shard_map/ppermute | solution.py:39
  27.7 13.0 %copy-start.10 = (bf16[16,6144]{1,0:T(8,128)(2,1)S(1)}, bf16[16,6144]{1,0:T(8,128)(2,1)}, u32[]{:S(2)}) copy-start(bf16[16,6144]{1,0:T(8,128)(2,1)} %param.18) | copy-start | bytes 589828
  28.7 12.7 %collective-permute-start.10 = (bf16[384,384]{1,0:T(8,128)(2,1)S(1)}, bf16[384,384]{1,0:T(8,128)(2,1)S(1)}, u32[]{:S(2)}, u32[]{:S(2)}) collective-permute-start(bf16[384,384]{1,0:T(8,128)(2,1)S(1)} %slice.55), channel_id=1, source_target_pairs={{0,48},{1,49},{2,50},{3,51},{4,52},{5,53},{6,54},{7,55},{8,56},{9,... | collective-permute-start | bytes 884744 | tf_op jit(solution)/shard_map/ppermute | solution.py:43
  30.9 10.5 %collective-permute-start.9 = (bf16[384,384]{1,0:T(8,128)(2,1)S(1)}, bf16[384,384]{1,0:T(8,128)(2,1)S(1)}, u32[]{:S(2)}, u32[]{:S(2)}) collective-permute-start(bf16[384,384]{1,0:T(8,128)(2,1)S(1)} %slice.54), channel_id=1, source_target_pairs={{0,16},{1,17},{2,18},{3,19},{4,20},{5,21},{6,22},{7,23},{8,24},{9,... | collective-permute-start | bytes 884744 | tf_op jit(solution)/shard_map/ppermute | solution.py:43
  30.9 0.9 copy-start.7
  37.6 8.4 %collective-permute-start.8 = (bf16[128,768]{1,0:T(8,128)(2,1)S(1)}, bf16[128,768]{1,0:T(8,128)(2,1)S(1)}, u32[]{:S(2)}, u32[]{:S(2)}) collective-permute-start(bf16[128,768]{1,0:T(8,128)(2,1)S(1)} %shard_map.128.block), channel_id=1, source_target_pairs={{0,64},{1,65},{2,66},{3,67},{4,68},{5,69},{6,70},{7,71},{8,72},{9,... | collective-permute-start | bytes 589832 | tf_op jit(solution)/shard_map/ppermute | solution.py:35
  46.1 2.1 collective-permute-start.11
  48.2 34.0 %collective-permute-start.15 = (bf16[6144,512]{1,0:T(8,128)(2,1)}, bf16[6144,512]{1,0:T(8,128)(2,1)}, u32[]{:S(2)}, u32[]{:S(2)}) collective-permute-start(bf16[6144,512]{1,0:T(8,128)(2,1)} %bitcast.56), channel_id=1, source_target_pairs={{0,8},{1,9},{2,10},{3,11},{4,12},{5,13},{6,14},{7,15},{8,0},{9,1},... | collective-permute-start | bytes 18874376 | tf_op jit(solution)/shard_map/ppermute | solution.py:39
  48.3 33.9 %collective-permute-start.16 = (bf16[6144,512]{1,0:T(8,128)(2,1)}, bf16[6144,512]{1,0:T(8,128)(2,1)}, u32[]{:S(2)}, u32[]{:S(2)}) collective-permute-start(bf16[6144,512]{1,0:T(8,128)(2,1)} %bitcast.70), channel_id=1, source_target_pairs={{0,8},{1,9},{2,10},{3,11},{4,12},{5,13},{6,14},{7,15},{8,0},{9,1},... | collective-permute-start | bytes 18874376 | tf_op jit(solution)/shard_map/ppermute | solution.py:39
  48.7 96.8 %collective-permute-start.25 = (bf16[512,6144]{1,0:T(8,128)(2,1)}, bf16[512,6144]{1,0:T(8,128)(2,1)}, u32[]{:S(2)}, u32[]{:S(2)}) collective-permute-start(bf16[512,6144]{1,0:T(8,128)(2,1)} %bitcast.59), channel_id=1, source_target_pairs={{0,8},{1,9},{2,10},{3,11},{4,12},{5,13},{6,14},{7,15},{8,0},{9,1},... | collective-permute-start | bytes 18874376 | tf_op jit(solution)/shard_map/ppermute | solution.py:39
  51.8 9.6 %copy-start.11 = (bf16[16,3072]{1,0:T(8,128)(2,1)S(1)}, bf16[16,3072]{1,0:T(8,128)(2,1)}, u32[]{:S(2)}) copy-start(bf16[16,3072]{1,0:T(8,128)(2,1)} %get-tuple-element.57) | copy-start | bytes 294916
  51.8 29.3 %copy-start.2 = (bf16[16,3072]{1,0:T(8,128)(2,1)S(1)}, bf16[16,3072]{1,0:T(8,128)(2,1)}, u32[]{:S(2)}) copy-start(bf16[16,3072]{1,0:T(8,128)(2,1)} %get-tuple-element.95.res_own) | copy-start | bytes 294916
  51.8 29.3 %all-to-all-start = ((bf16[8,32,3072]{2,1,0:T(8,128)(2,1)}), bf16[8,32,3072]{2,1,0:T(8,128)(2,1)S(1)}, u32[]{:S(2)}, u32[]{:S(2)}) async-start(bf16[8,32,3072]{2,1,0:T(8,128)(2,1)} %shard_map.129), calls=%async_computation | async-start | bytes 3145728 | tf_op jit(solution)/shard_map/all_to_all | solution.py:488
  58.6 20.9 %collective-permute-start.13 = (s32[32]{0:T(128)S(1)}, s32[32]{0:T(128)S(1)}, u32[]{:S(2)}, u32[]{:S(2)}) collective-permute-start(s32[32]{0:T(128)S(1)} %reshape.31), channel_id=1, source_target_pairs={{0,64},{1,65},{2,66},{3,67},{4,68},{5,69},{6,70},{7,71},{8,72},{9,... | collective-permute-start | bytes 392 | tf_op jit(solution)/shard_map/ppermute | solution.py:35
  61.3 19.7 %collective-permute-start.12 = (bf16[16,3072]{1,0:T(8,128)(2,1)S(1)}, bf16[16,3072]{1,0:T(8,128)(2,1)S(1)}, u32[]{:S(2)}, u32[]{:S(2)}) collective-permute-start(bf16[16,3072]{1,0:T(8,128)(2,1)S(1)} %copy-done.11), channel_id=1, source_target_pairs={{0,64},{1,65},{2,66},{3,67},{4,68},{5,69},{6,70},{7,71},{8,72},{9,... | collective-permute-start | bytes 294920 | tf_op jit(solution)/shard_map/ppermute | solution.py:35
  99.1 33.8 %copy-start.12 = (bf16[6144]{0:T(1024)(128)(2,1)S(1)}, bf16[6144]{0:T(1024)(128)(2,1)}, u32[]{:S(2)}) copy-start(bf16[6144]{0:T(1024)(128)(2,1)} %param.20) | copy-start | bytes 36868
  99.1 33.8 %dynamic-slice-start = ((bf16[6144]{0:T(1024)(128)(2,1)}, s32[]{:T(128)}), bf16[3072]{0:T(1024)(128)(2,1)S(1)}, s32[]{:S(2)}) async-start(bf16[6144]{0:T(1024)(128)(2,1)} %param.20, s32[]{:T(128)} %select_n.82), calls=%async_computation.3 | async-start | bytes 12800 | tf_op jit(solution)/shard_map/dynamic-slice
  99.1 18.0 %collective-permute-start.20 = (bf16[128,3072]{1,0:T(8,128)(2,1)S(1)}, bf16[128,3072]{1,0:T(8,128)(2,1)S(1)}, u32[]{:S(2)}, u32[]{:S(2)}) collective-permute-start(bf16[128,3072]{1,0:T(8,128)(2,1)S(1)} %bitcast.62), channel_id=1, source_target_pairs={{0,16},{1,17},{2,18},{3,19},{4,20},{5,21},{6,22},{7,23},{8,24},{9,... | collective-permute-start | bytes 2359304 | tf_op jit(solution)/shard_map/ppermute | solution.py:43
  99.7 17.6 %collective-permute-start.22 = (bf16[128,3072]{1,0:T(8,128)(2,1)S(1)}, bf16[128,3072]{1,0:T(8,128)(2,1)S(1)}, u32[]{:S(2)}, u32[]{:S(2)}) collective-permute-start(bf16[128,3072]{1,0:T(8,128)(2,1)S(1)} %bitcast.63), channel_id=1, source_target_pairs={{0,48},{1,49},{2,50},{3,51},{4,52},{5,53},{6,54},{7,55},{8,56},{9,... | collective-permute-start | bytes 2359304 | tf_op jit(solution)/shard_map/ppermute | solution.py:43
  102.3 18.3 %collective-permute-start.17 = (bf16[128,3072]{1,0:T(8,128)(2,1)S(1)}, bf16[128,3072]{1,0:T(8,128)(2,1)S(1)}, u32[]{:S(2)}, u32[]{:S(2)}) collective-permute-start(bf16[128,3072]{1,0:T(8,128)(2,1)S(1)} %bitcast.64), channel_id=1, source_target_pairs={{0,64},{1,65},{2,66},{3,67},{4,68},{5,69},{6,70},{7,71},{8,72},{9,... | collective-permute-start | bytes 2359304 | tf_op jit(solution)/shard_map/ppermute | solution.py:35
  117.2 13.3 %collective-permute-start.21 = (bf16[64,3072]{1,0:T(8,128)(2,1)S(1)}, bf16[64,3072]{1,0:T(8,128)(2,1)S(1)}, u32[]{:S(2)}, u32[]{:S(2)}) collective-permute-start(bf16[64,3072]{1,0:T(8,128)(2,1)S(1)} %slice.72), channel_id=1, source_target_pairs={{0,16},{1,17},{2,18},{3,19},{4,20},{5,21},{6,22},{7,23},{8,24},{9,... | collective-permute-start | bytes 1179656 | tf_op jit(solution)/shard_map/ppermute | solution.py:43
  117.3 13.2 %collective-permute-start.23 = (bf16[64,3072]{1,0:T(8,128)(2,1)S(1)}, bf16[64,3072]{1,0:T(8,128)(2,1)S(1)}, u32[]{:S(2)}, u32[]{:S(2)}) collective-permute-start(bf16[64,3072]{1,0:T(8,128)(2,1)S(1)} %slice.73), channel_id=1, source_target_pairs={{0,48},{1,49},{2,50},{3,51},{4,52},{5,53},{6,54},{7,55},{8,56},{9,... | collective-permute-start | bytes 1179656 | tf_op jit(solution)/shard_map/ppermute | solution.py:43
  120.6 24.9 %collective-permute-start.18 = (bf16[128,3072]{1,0:T(8,128)(2,1)S(1)}, bf16[128,3072]{1,0:T(8,128)(2,1)S(1)}, u32[]{:S(2)}, u32[]{:S(2)}) collective-permute-start(bf16[128,3072]{1,0:T(8,128)(2,1)S(1)} %collective-permute-done.17.near), channel_id=1, source_target_pairs={{0,48},{1,49},{2,50},{3,51},{4,52},{5,53},{6,54},{7,55},{8,56},{9,... | collective-permute-start | bytes 2359304 | tf_op jit(solution)/shard_map/ppermute | solution.py:43
  121.8 23.7 %collective-permute-start.19 = (bf16[128,3072]{1,0:T(8,128)(2,1)S(1)}, bf16[128,3072]{1,0:T(8,128)(2,1)S(1)}, u32[]{:S(2)}, u32[]{:S(2)}) collective-permute-start(bf16[128,3072]{1,0:T(8,128)(2,1)S(1)} %collective-permute-done.17.near), channel_id=1, source_target_pairs={{0,16},{1,17},{2,18},{3,19},{4,20},{5,21},{6,22},{7,23},{8,24},{9,... | collective-permute-start | bytes 2359304 | tf_op jit(solution)/shard_map/ppermute | solution.py:43
  130.6 15.0 %collective-permute-start.24 = (bf16[128,3072]{1,0:T(8,128)(2,1)S(1)}, bf16[128,3072]{1,0:T(8,128)(2,1)S(1)}, u32[]{:S(2)}, u32[]{:S(2)}) collective-permute-start(bf16[128,3072]{1,0:T(8,128)(2,1)S(1)} %constant_dynamic-update-slice_fusion.10.far), channel_id=1, source_target_pairs={{0,64},{1,65},{2,66},{3,67},{4,68},{5,69},{6,70},{7,71},{8,72},{9,... | collective-permute-start | bytes 2359304 | tf_op jit(solution)/shard_map/ppermute | solution.py:35
  133.0 2.8 %copy-start = (bf16[1,6144,512]{2,1,0:T(8,128)(2,1)S(1)}, bf16[1,6144,512]{2,1,0:T(8,128)(2,1)}, u32[]{:S(2)}) copy-start(bf16[1,6144,512]{2,1,0:T(8,128)(2,1)} %param.21) | copy-start | bytes 18874372
  145.5 17.1 %copy-start.13 = (f32[16,2]{0,1:T(2,128)S(1)}, f32[16,2]{0,1:T(2,128)}, u32[]{:S(2)}) copy-start(f32[16,2]{0,1:T(2,128)} %param.25) | copy-start | bytes 388
  161.0 16.2 %collective-permute-start.29 = (bf16[64,6144]{1,0:T(8,128)(2,1)}, bf16[64,6144]{1,0:T(8,128)(2,1)}, u32[]{:S(2)}, u32[]{:S(2)}) collective-permute-start(bf16[64,6144]{1,0:T(8,128)(2,1)} %get-tuple-element.82), channel_id=1, source_target_pairs={{0,64},{1,65},{2,66},{3,67},{4,68},{5,69},{6,70},{7,71},{8,72},{9,... | collective-permute-start | bytes 2359304 | tf_op jit(solution)/shard_map/ppermute | solution.py:35
  162.7 18.0 %collective-permute-start.26 = (bf16[64,6144]{1,0:T(8,128)(2,1)S(1)}, bf16[64,6144]{1,0:T(8,128)(2,1)S(1)}, u32[]{:S(2)}, u32[]{:S(2)}) collective-permute-start(bf16[64,6144]{1,0:T(8,128)(2,1)S(1)} %get-tuple-element.75), channel_id=1, source_target_pairs={{0,16},{1,17},{2,18},{3,19},{4,20},{5,21},{6,22},{7,23},{8,24},{9,... | collective-permute-start | bytes 2359304 | tf_op jit(solution)/shard_map/ppermute | solution.py:43
  163.4 17.2 %collective-permute-start.27 = (bf16[64,6144]{1,0:T(8,128)(2,1)S(1)}, bf16[64,6144]{1,0:T(8,128)(2,1)S(1)}, u32[]{:S(2)}, u32[]{:S(2)}) collective-permute-start(bf16[64,6144]{1,0:T(8,128)(2,1)S(1)} %get-tuple-element.76), channel_id=1, source_target_pairs={{0,48},{1,49},{2,50},{3,51},{4,52},{5,53},{6,54},{7,55},{8,56},{9,... | collective-permute-start | bytes 2359304 | tf_op jit(solution)/shard_map/ppermute | solution.py:43
  166.4 2.8 %copy-start.1 = (bf16[1,512,6144]{2,1,0:T(8,128)(2,1)S(1)}, bf16[1,512,6144]{2,1,0:T(8,128)(2,1)}, u32[]{:S(2)}) copy-start(bf16[1,512,6144]{2,1,0:T(8,128)(2,1)} %param.23) | copy-start | bytes 18874372
  178.5 12.1 %collective-permute-start.32 = (bf16[64,3072]{1,0:T(8,128)(2,1)S(1)}, bf16[64,3072]{1,0:T(8,128)(2,1)S(1)}, u32[]{:S(2)}, u32[]{:S(2)}) collective-permute-start(bf16[64,3072]{1,0:T(8,128)(2,1)S(1)} %get-tuple-element.91), channel_id=1, source_target_pairs={{0,48},{1,49},{2,50},{3,51},{4,52},{5,53},{6,54},{7,55},{8,56},{9,... | collective-permute-start | bytes 1179656 | tf_op jit(solution)/shard_map/ppermute | solution.py:43
  180.3 13.4 %collective-permute-start.30 = (bf16[64,3072]{1,0:T(8,128)(2,1)S(1)}, bf16[64,3072]{1,0:T(8,128)(2,1)S(1)}, u32[]{:S(2)}, u32[]{:S(2)}) collective-permute-start(bf16[64,3072]{1,0:T(8,128)(2,1)S(1)} %get-tuple-element.92), channel_id=1, source_target_pairs={{0,16},{1,17},{2,18},{3,19},{4,20},{5,21},{6,22},{7,23},{8,24},{9,... | collective-permute-start | bytes 1179656 | tf_op jit(solution)/shard_map/ppermute | solution.py:43
  180.9 22.0 %collective-permute-start.28 = (bf16[64,6144]{1,0:T(8,128)(2,1)S(1)}, bf16[64,6144]{1,0:T(8,128)(2,1)S(1)}, u32[]{:S(2)}, u32[]{:S(2)}) collective-permute-start(bf16[64,6144]{1,0:T(8,128)(2,1)S(1)} %add_convert_fusion), channel_id=1, source_target_pairs={{0,64},{1,65},{2,66},{3,67},{4,68},{5,69},{6,70},{7,71},{8,72},{9,... | collective-permute-start | bytes 2359304 | tf_op jit(solution)/shard_map/ppermute | solution.py:35
  183.0 19.9 %collective-permute-start.34 = (bf16[64,3072]{1,0:T(8,128)(2,1)S(1)}, bf16[64,3072]{1,0:T(8,128)(2,1)S(1)}, u32[]{:S(2)}, u32[]{:S(2)}) collective-permute-start(bf16[64,3072]{1,0:T(8,128)(2,1)S(1)} %get-tuple-element.85), channel_id=1, source_target_pairs={{0,48},{1,49},{2,50},{3,51},{4,52},{5,53},{6,54},{7,55},{8,56},{9,... | collective-permute-start | bytes 1179656 | tf_op jit(solution)/shard_map/ppermute | solution.py:43
  185.9 17.0 %collective-permute-start.35 = (bf16[64,3072]{1,0:T(8,128)(2,1)S(1)}, bf16[64,3072]{1,0:T(8,128)(2,1)S(1)}, u32[]{:S(2)}, u32[]{:S(2)}) collective-permute-start(bf16[64,3072]{1,0:T(8,128)(2,1)S(1)} %get-tuple-element.87), channel_id=1, source_target_pairs={{0,16},{1,17},{2,18},{3,19},{4,20},{5,21},{6,22},{7,23},{8,24},{9,... | collective-permute-start | bytes 1179656 | tf_op jit(solution)/shard_map/ppermute | solution.py:43
  190.8 10.4 %collective-permute-start.33 = (bf16[64,3072]{1,0:T(8,128)(2,1)S(1)}, bf16[64,3072]{1,0:T(8,128)(2,1)S(1)}, u32[]{:S(2)}, u32[]{:S(2)}) collective-permute-start(bf16[64,3072]{1,0:T(8,128)(2,1)S(1)} %add_convert_fusion.3), channel_id=1, source_target_pairs={{0,48},{1,49},{2,50},{3,51},{4,52},{5,53},{6,54},{7,55},{8,56},{9,... | collective-permute-start | bytes 1179656 | tf_op jit(solution)/shard_map/ppermute | solution.py:43
  193.8 9.1 %collective-permute-start.31 = (bf16[64,3072]{1,0:T(8,128)(2,1)S(1)}, bf16[64,3072]{1,0:T(8,128)(2,1)S(1)}, u32[]{:S(2)}, u32[]{:S(2)}) collective-permute-start(bf16[64,3072]{1,0:T(8,128)(2,1)S(1)} %add_convert_fusion.5), channel_id=1, source_target_pairs={{0,16},{1,17},{2,18},{3,19},{4,20},{5,21},{6,22},{7,23},{8,24},{9,... | collective-permute-start | bytes 1179656 | tf_op jit(solution)/shard_map/ppermute | solution.py:43
  204.3 15.3 %all-to-all-start.2 = ((bf16[8,8,6144]{2,1,0:T(8,128)(2,1)}), bf16[8,8,6144]{2,1,0:T(8,128)(2,1)S(1)}, u32[]{:S(2)}, u32[]{:S(2)}) async-start(bf16[8,8,6144]{2,1,0:T(8,128)(2,1)} %maximum_bitcast_fusion), calls=%async_computation.2 | async-start | bytes 1572864 | tf_op jit(solution)/shard_map/all_to_all | solution.py:558
  210.1 9.7 %collective-permute-start.14 = (bf16[16,3072]{1,0:T(8,128)(2,1)S(1)}, bf16[16,3072]{1,0:T(8,128)(2,1)S(1)}, u32[]{:S(2)}, u32[]{:S(2)}) collective-permute-start(bf16[16,3072]{1,0:T(8,128)(2,1)S(1)} %get-tuple-element.94), channel_id=1, source_target_pairs={{0,64},{1,65},{2,66},{3,67},{4,68},{5,69},{6,70},{7,71},{8,72},{9,... | collective-permute-start | bytes 294920 | tf_op jit(solution)/shard_map/ppermute | solution.py:35

commit v2 on v1

--- a/solution.py
+++ b/solution.py
@@ -61,7 +61,7 @@
 
 STEPS = (0, 1, -1, 2)
 INNER = 2
-OUTER = 4
+OUTER = 2
 
 
 def pack(k_load, v_load, scales, docs, out, keys, values, sems):
@@ -434,6 +434,31 @@
     )(hidden, own, other)
 
 
+def settle(own, cross, free_above, last_below, free_below, last_above, out):
+    half = free_above.shape[1]
+    for columns, free, last in (
+        (slice(0, half), free_above, last_below),
+        (slice(half, 2 * half), free_below, last_above),
+    ):
+        total = own[:, columns].astype(F32) + cross[:, columns].astype(F32)
+        total = total + free[...].astype(F32) + last[...].astype(F32)
+        out[:, columns] = total.astype(BF16)
+
+
+def last_sum(*terms):
+    vmem = pl.BlockSpec(memory_space=pltpu.VMEM)
+    return pl.pallas_call(
+        settle,
+        out_shape=jax.ShapeDtypeStruct(terms[0].shape, BF16),
+        in_specs=[vmem] * len(terms),
+        out_specs=vmem,
+        compiler_params=pltpu.CompilerParams(vmem_limit_bytes=16 * 2**20),
+        cost_estimate=pl.CostEstimate(
+            flops=4 * terms[0].size, bytes_accessed=10 * terms[0].size, transcendentals=0
+        ),
+    )(*terms)
+
+
 def per_device(
     queries,
     k_load,
@@ -547,13 +572,7 @@
     from_cross, last_below, last_above = lax.optimization_barrier(
         (from_cross, last_below, last_above)
     )
-    expert_out = jnp.concatenate(
-        [
-            added(own[:, :half], from_cross[:, :half], free_above, last_below),
-            added(own[:, half:], from_cross[:, half:], free_below, last_above),
-        ],
-        1,
-    )
+    expert_out = last_sum(own, from_cross, free_above, last_below, free_below, last_above)
 
     returned = lax.all_to_all(
         expert_out.reshape(NE, CAP, width), "exp", split_axis=0, concat_axis=0, tiled=True

time: 222 us -> 221 us (level)
  transfers between devices with their start and end apart: 38 -> 38, of which waited for: 14 -> 14; matrix products, arithmetic and copies ran while one was open for 5% -> 5% of each run, Pallas kernels for 12% -> 13%
where the time goes in v2:
time: 221 us; the launch traced here: 220 us
  waiting for transfers between devices  73.6 us (33%)
  starting transfers between devices  63.4 us (29%)
  Pallas kernels  44.2 us (20%)
  local copies, waits for them, and re-layouts  18 us (8%)
  blocking collectives  16.9 us (8%)
  other arithmetic  2.46 us (1%)
    ppermute x21, waiting for transfers between devices, from_y(): return lax.ppermute(value, BOTH, partner(step_y=-step))  38.1 us
    ppermute x21, starting transfers between devices, from_y(): return lax.ppermute(value, BOTH, partner(step_y=-step))  29.9 us
    ppermute x9, waiting for transfers between devices, flip_x(): return lax.ppermute(value, BOTH, partner(flip_x=1))  26.8 us
    ppermute x9, starting transfers between devices, flip_x(): return lax.ppermute(value, BOTH, partner(flip_x=1))  20.6 us
    all_to_all x1, blocking collectives, per_device(): lax.all_to_all(outgoing.reshape(NE, 2 * CAP, half), 'exp', split_axis=0,...  16.9 us
    pallas_call x1, Pallas kernels, expert_rest(): pl.pallas_call(finish, out_shape=[jax.ShapeDtypeStruct((2, NY, rows // 2,...  15 us
    unnamed x39, local copies, waits for them, and re-layouts  13.8 us
    pallas_call x1, Pallas kernels, expert_in(): pl.pallas_call(begin, grid_spec=pltpu.PrefetchScalarGridSpec(num_scalar_p...  9.66 us
  transfers between devices with their start and end apart: 38, of which 14 were waited for; matrix products, arithmetic and copies ran while one was open for 5% of the time, Pallas kernels for 13%

profile of v2, /device:TPU:0, one launch (start us, length us, event | category | flops | bytes accessed | tf_op | source)
XLA Modules:
  0.0 220.2 jit_solution(11779942962249535088)
XLA Ops:
  0.0 0.8 copy-done.3
  0.8 0.8 copy-done.4
  1.5 0.7 copy-done.5
  2.2 0.7 copy-done.6
  3.2 3.2 %collective-permute-start = (bf16[144,256]{1,0:T(8,128)(2,1)S(1)}, bf16[144,256]{1,0:T(8,128)(2,1)S(1)}, u32[]{:S(2)}, u32[]{:S(2)}) collective-permute-start(bf16[144,256]{1,0:T(8,128)(2,1)S(1)} %shard_map.127), channel_id=1, source_target_pairs={{0,48},{1,49},{2,50},{3,51},{4,52},{5,53},{6,54},{7,55},{8,56},{9,... | collective-permute-start | bytes 221192 | tf_op jit(solution)/shard_map/ppermute | solution.py:43
  6.4 2.2 %collective-permute-start.2 = (bf16[144,256]{1,0:T(8,128)(2,1)S(1)}, bf16[144,256]{1,0:T(8,128)(2,1)S(1)}, u32[]{:S(2)}, u32[]{:S(2)}) collective-permute-start(bf16[144,256]{1,0:T(8,128)(2,1)S(1)} %shard_map.127), channel_id=1, source_target_pairs={{0,32},{1,33},{2,34},{3,35},{4,36},{5,37},{6,38},{7,39},{8,40},{9,... | collective-permute-start | bytes 221192 | tf_op jit(solution)/shard_map/ppermute | solution.py:43
  8.6 1.1 collective-permute-start.4
  9.6 1.0 collective-permute-start.5
  10.6 0.6 constant_dynamic-update-slice_fusion.4
  11.2 1.1 constant_dynamic-update-slice_fusion.7
  12.4 0.8 collective-permute-done.1
  13.2 3.1 %collective-permute-start.3 = (bf16[4,144,256]{2,1,0:T(8,128)(2,1)S(1)}, bf16[4,144,256]{2,1,0:T(8,128)(2,1)S(1)}, u32[]{:S(2)}, u32[]{:S(2)}) collective-permute-start(bf16[4,144,256]{2,1,0:T(8,128)(2,1)S(1)} %pad_maximum_fusion), channel_id=1, source_target_pairs={{0,64},{1,65},{2,66},{3,67},{4,68},{5,69},{6,70},{7,71},{8,72},{9,... | collective-permute-start | bytes 884744 | tf_op jit(solution)/shard_map/ppermute | solution.py:35
  16.3 0.6 constant_dynamic-update-slice_fusion.3
  16.9 0.6 constant_dynamic-update-slice_fusion.2
  18.2 3.7 %collective-permute-done.3 = bf16[4,144,256]{2,1,0:T(8,128)(2,1)S(1)} collective-permute-done((bf16[4,144,256]{2,1,0:T(8,128)(2,1)S(1)}, bf16[4,144,256]{2,1,0:T(8,128)(2,1)S(1)}, u32[]{:S(2)}, u32[]{:S(2)}) %collective-permute-start.3) | collective-permute-done | bytes 294944 | tf_op jit(solution)/shard_map/ppermute | solution.py:35
  21.9 0.7 constant_dynamic-update-slice_fusion.mine
  22.6 1.9 collective-permute-done.4
  24.5 1.0 collective-permute-done.5
  26.7 1.0 slice.43
  27.7 1.0 slice.42
  28.7 2.1 collective-permute-start.10
  30.9 0.9 copy-done.7
  31.8 5.8 %shard_map.128.block = bf16[128,768]{1,0:T(8,128)(2,1)S(1)} custom-call(s32[16]{0:T(128)S(1)} %stack.103.start, bf16[128,768]{1,0:T(8,128)(2,1)S(1)} %copy-done.7, bf16[8,144,256]{2,1,0:T(8,128)(2,1)} %constant_dynamic-update-slice_fusion.mine, bf16[8,144,256]{2,1,0:T(8,128)(2,1)} %collective-permute-done.6.other), custom_call_target="tpu_custom_call" | custom-call | flops 805306368 | bytes 1600000 | tf_op jit(solution)/shard_map/pallas_call | solution.py:154
  37.6 3.1 %collective-permute-start.8 = (bf16[128,768]{1,0:T(8,128)(2,1)S(1)}, bf16[128,768]{1,0:T(8,128)(2,1)S(1)}, u32[]{:S(2)}, u32[]{:S(2)}) collective-permute-start(bf16[128,768]{1,0:T(8,128)(2,1)S(1)} %shard_map.128.block), channel_id=1, source_target_pairs={{0,64},{1,65},{2,66},{3,67},{4,68},{5,69},{6,70},{7,71},{8,72},{9,... | collective-permute-start | bytes 589832 | tf_op jit(solution)/shard_map/ppermute | solution.py:35
  40.7 0.7 constant_dynamic-slice_fusion
  41.4 4.6 %collective-permute-done.8.across = bf16[128,768]{1,0:T(8,128)(2,1)S(1)} collective-permute-done((bf16[128,768]{1,0:T(8,128)(2,1)S(1)}, bf16[128,768]{1,0:T(8,128)(2,1)S(1)}, u32[]{:S(2)}, u32[]{:S(2)}) %collective-permute-start.8) | collective-permute-done | bytes 196640 | tf_op jit(solution)/shard_map/ppermute | solution.py:35
  46.2 2.0 collective-permute-done.11.far_other
  48.8 2.9 %shard_map.129 = bf16[8,32,3072]{2,1,0:T(8,128)(2,1)} custom-call(bf16[128,768]{1,0:T(8,128)(2,1)S(1)} %shard_map.128.block, bf16[128,768]{1,0:T(8,128)(2,1)S(1)} %collective-permute-done.8.across, bf16[768,1152]{1,0:T(8,128)(2,1)S(1)} %constant_dynamic-update-slice_fusion.5.near, bf16[768,384]{1,0:T(8,128)(2,1)S(1)} %constant_dynamic-update-slice_fusion.8.far, ...), custom_call_target="tpu_custom_call" | custom-call | flops 1207959552 | bytes 6500000 | tf_op jit(solution)/shard_map/pallas_call | solution.py:182
  51.8 6.4 %all-to-all-start = ((bf16[8,32,3072]{2,1,0:T(8,128)(2,1)}), bf16[8,32,3072]{2,1,0:T(8,128)(2,1)S(1)}, u32[]{:S(2)}, u32[]{:S(2)}) async-start(bf16[8,32,3072]{2,1,0:T(8,128)(2,1)} %shard_map.129), calls=%async_computation | async-start | bytes 3145728 | tf_op jit(solution)/shard_map/all_to_all | solution.py:513
  58.6 2.8 %collective-permute-start.13 = (s32[32]{0:T(128)S(1)}, s32[32]{0:T(128)S(1)}, u32[]{:S(2)}, u32[]{:S(2)}) collective-permute-start(s32[32]{0:T(128)S(1)} %reshape.31), channel_id=1, source_target_pairs={{0,64},{1,65},{2,66},{3,67},{4,68},{5,69},{6,70},{7,71},{8,72},{9,... | collective-permute-start | bytes 392 | tf_op jit(solution)/shard_map/ppermute | solution.py:35
  61.3 0.8 collective-permute-start.12
  62.1 17.3 %collective-permute-done.13 = s32[32]{0:T(128)S(1)} collective-permute-done((s32[32]{0:T(128)S(1)}, s32[32]{0:T(128)S(1)}, u32[]{:S(2)}, u32[]{:S(2)}) %collective-permute-start.13) | collective-permute-done | bytes 160 | tf_op jit(solution)/shard_map/ppermute | solution.py:35
  79.9 1.1 collective-permute-done.12.res_across
  81.1 1.1 shard_map.130
  82.2 16.9 %all_to_all.15 = bf16[8,16,3072]{2,1,0:T(8,128)(2,1)S(1)} all-to-all(bf16[8,16,3072]{2,1,0:T(8,128)(2,1)S(1)} %bitcast.65), channel_id=1, replica_groups=mesh['ctx'=16,'exp'=8] {'exp'}, dimensions={0} | all-to-all | bytes 1572864 | tf_op jit(solution)/shard_map/all_to_all | solution.py:527
  99.7 2.7 %collective-permute-start.22 = (bf16[128,3072]{1,0:T(8,128)(2,1)S(1)}, bf16[128,3072]{1,0:T(8,128)(2,1)S(1)}, u32[]{:S(2)}, u32[]{:S(2)}) collective-permute-start(bf16[128,3072]{1,0:T(8,128)(2,1)S(1)} %bitcast.62), channel_id=1, source_target_pairs={{0,48},{1,49},{2,50},{3,51},{4,52},{5,53},{6,54},{7,55},{8,56},{9,... | collective-permute-start | bytes 2359304 | tf_op jit(solution)/shard_map/ppermute | solution.py:43
  102.3 2.0 collective-permute-start.17
  104.3 12.8 %collective-permute-done.20.below = bf16[128,3072]{1,0:T(8,128)(2,1)S(1)} collective-permute-done((bf16[128,3072]{1,0:T(8,128)(2,1)S(1)}, bf16[128,3072]{1,0:T(8,128)(2,1)S(1)}, u32[]{:S(2)}, u32[]{:S(2)}) %collective-permute-start.20) | collective-permute-done | bytes 786464 | tf_op jit(solution)/shard_map/ppermute | solution.py:43
  117.3 3.3 %collective-permute-start.23 = (bf16[64,3072]{1,0:T(8,128)(2,1)S(1)}, bf16[64,3072]{1,0:T(8,128)(2,1)S(1)}, u32[]{:S(2)}, u32[]{:S(2)}) collective-permute-start(bf16[64,3072]{1,0:T(8,128)(2,1)S(1)} %slice.57), channel_id=1, source_target_pairs={{0,48},{1,49},{2,50},{3,51},{4,52},{5,53},{6,54},{7,55},{8,56},{9,... | collective-permute-start | bytes 1179656 | tf_op jit(solution)/shard_map/ppermute | solution.py:43
  120.6 1.2 collective-permute-start.18
  121.8 0.8 collective-permute-start.19
  122.6 7.9 %collective-permute-done.21 = bf16[64,3072]{1,0:T(8,128)(2,1)S(1)} collective-permute-done((bf16[64,3072]{1,0:T(8,128)(2,1)S(1)}, bf16[64,3072]{1,0:T(8,128)(2,1)S(1)}, u32[]{:S(2)}, u32[]{:S(2)}) %collective-permute-start.21) | collective-permute-done | bytes 393248 | tf_op jit(solution)/shard_map/ppermute | solution.py:43
  130.6 2.3 %collective-permute-start.24 = (bf16[128,3072]{1,0:T(8,128)(2,1)S(1)}, bf16[128,3072]{1,0:T(8,128)(2,1)S(1)}, u32[]{:S(2)}, u32[]{:S(2)}) collective-permute-start(bf16[128,3072]{1,0:T(8,128)(2,1)S(1)} %constant_dynamic-update-slice_fusion.10.far), channel_id=1, source_target_pairs={{0,64},{1,65},{2,66},{3,67},{4,68},{5,69},{6,70},{7,71},{8,72},{9,... | collective-permute-start | bytes 2359304 | tf_op jit(solution)/shard_map/ppermute | solution.py:35
  133.0 2.8 %copy-done = bf16[1,6144,512]{2,1,0:T(8,128)(2,1)S(1)} copy-done((bf16[1,6144,512]{2,1,0:T(8,128)(2,1)S(1)}, bf16[1,6144,512]{2,1,0:T(8,128)(2,1)}, u32[]{:S(2)}) %copy-start) | copy-done | bytes 6291480
  135.8 9.7 %shard_map.131 = (f32[4,512,512]{2,1,0:T(8,128)S(1)}, f32[512,128]{1,0:T(8,128)S(1)}) custom-call(s32[1]{0:T(128)} %bitcast.32.which, bf16[128,3072]{1,0:T(8,128)(2,1)S(1)} %bitcast.64, bf16[128,3072]{1,0:T(8,128)(2,1)S(1)} %collective-permute-done.22.above, bf16[128,3072]{1,0:T(8,128)(2,1)S(1)} %collective-permute-done.20.below, ...), custom_call_target="tpu_custom_call" | custom-call | flops 6442450944 | bytes 16000000 | tf_op jit(solution)/shard_map/pallas_call | solution.py:359
  145.6 15.0 %shard_map.132 = (bf16[2,4,64,1024]{3,2,1,0:T(8,128)(2,1)S(1)}, bf16[64,6144]{1,0:T(8,128)(2,1)S(1)}, bf16[64,6144]{1,0:T(8,128)(2,1)S(1)}, bf16[64,6144]{1,0:T(8,128)(2,1)}) custom-call(s32[2]{0:T(128)S(1)} %pad_add_fusion.1.which, bf16[128,3072]{1,0:T(8,128)(2,1)S(1)} %collective-permute-done.17.near, bf16[128,3072]{1,0:T(8,128)(2,1)S(1)} %collective-permute-done.18.above, ...), custom_call_target="tpu_custom_call" | custom-call | flops 9663676416 | bytes 26000000 | tf_op jit(solution)/shard_map/pallas_call | solution.py:332
  160.5 1.6 collective-permute-start.29
  162.2 0.8 collective-permute-start.26
  162.9 2.9 %collective-permute-start.27 = (bf16[64,6144]{1,0:T(8,128)(2,1)S(1)}, bf16[64,6144]{1,0:T(8,128)(2,1)S(1)}, u32[]{:S(2)}, u32[]{:S(2)}) collective-permute-start(bf16[64,6144]{1,0:T(8,128)(2,1)S(1)} %get-tuple-element.76), channel_id=1, source_target_pairs={{0,48},{1,49},{2,50},{3,51},{4,52},{5,53},{6,54},{7,55},{8,56},{9,... | collective-permute-start | bytes 2359304 | tf_op jit(solution)/shard_map/ppermute | solution.py:43
  165.9 2.8 %copy-done.1 = bf16[1,512,6144]{2,1,0:T(8,128)(2,1)S(1)} copy-done((bf16[1,512,6144]{2,1,0:T(8,128)(2,1)S(1)}, bf16[1,512,6144]{2,1,0:T(8,128)(2,1)}, u32[]{:S(2)}) %copy-start.1) | copy-done | bytes 6291480
  168.6 8.1 %shard_map.133 = (bf16[64,3072]{1,0:T(8,128)(2,1)S(1)}, bf16[64,3072]{1,0:T(8,128)(2,1)S(1)}, bf16[64,3072]{1,0:T(8,128)(2,1)S(1)}, bf16[64,3072]{1,0:T(8,128)(2...) custom-call(bf16[2,4,64,1024]{3,2,1,0:T(8,128)(2,1)S(1)} %get-tuple-element.72.hid, ...), custom_call_target="tpu_custom_call" | custom-call | flops 4026531840 | bytes 15000000 | tf_op jit(solution)/shard_map/pallas_call | solution.py:420
  176.7 1.3 add_convert_fusion.2
  178.0 1.8 collective-permute-start.32
  180.4 2.1 collective-permute-start.28
  182.5 2.9 %collective-permute-start.34 = (bf16[64,3072]{1,0:T(8,128)(2,1)S(1)}, bf16[64,3072]{1,0:T(8,128)(2,1)S(1)}, u32[]{:S(2)}, u32[]{:S(2)}) collective-permute-start(bf16[64,3072]{1,0:T(8,128)(2,1)S(1)} %get-tuple-element.85), channel_id=1, source_target_pairs={{0,48},{1,49},{2,50},{3,51},{4,52},{5,53},{6,54},{7,55},{8,56},{9,... | collective-permute-start | bytes 1179656 | tf_op jit(solution)/shard_map/ppermute | solution.py:43
  185.4 4.7 %collective-permute-done.32 = bf16[64,3072]{1,0:T(8,128)(2,1)S(1)} collective-permute-done((bf16[64,3072]{1,0:T(8,128)(2,1)S(1)}, bf16[64,3072]{1,0:T(8,128)(2,1)S(1)}, u32[]{:S(2)}, u32[]{:S(2)}) %collective-permute-start.32) | collective-permute-done | bytes 393248 | tf_op jit(solution)/shard_map/ppermute | solution.py:43
  190.2 3.0 %collective-permute-start.33 = (bf16[64,3072]{1,0:T(8,128)(2,1)S(1)}, bf16[64,3072]{1,0:T(8,128)(2,1)S(1)}, u32[]{:S(2)}, u32[]{:S(2)}) collective-permute-start(bf16[64,3072]{1,0:T(8,128)(2,1)S(1)} %add_convert_fusion.1), channel_id=1, source_target_pairs={{0,48},{1,49},{2,50},{3,51},{4,52},{5,53},{6,54},{7,55},{8,56},{9,... | collective-permute-start | bytes 1179656 | tf_op jit(solution)/shard_map/ppermute | solution.py:43
  193.4 7.2 %collective-permute-done.33.last_above = bf16[64,3072]{1,0:T(8,128)(2,1)S(1)} collective-permute-done((bf16[64,3072]{1,0:T(8,128)(2,1)S(1)}, bf16[64,3072]{1,0:T(8,128)(2,1)S(1)}, u32[]{:S(2)}, u32[]{:S(2)}) %collective-permute-start.33) | collective-permute-done | bytes 393248 | tf_op jit(solution)/shard_map/ppermute | solution.py:43
  200.6 1.7 collective-permute-done.31.last_below
  202.4 1.3 shard_map.134
  203.7 5.8 %all-to-all-start.2 = ((bf16[8,8,6144]{2,1,0:T(8,128)(2,1)}), bf16[8,8,6144]{2,1,0:T(8,128)(2,1)S(1)}, u32[]{:S(2)}, u32[]{:S(2)}) async-start(bf16[8,8,6144]{2,1,0:T(8,128)(2,1)} %bitcast.35), calls=%async_computation.2 | async-start | bytes 1572864 | tf_op jit(solution)/shard_map/all_to_all | solution.py:577
  209.5 2.8 %collective-permute-start.14 = (bf16[16,3072]{1,0:T(8,128)(2,1)S(1)}, bf16[16,3072]{1,0:T(8,128)(2,1)S(1)}, u32[]{:S(2)}, u32[]{:S(2)}) collective-permute-start(bf16[16,3072]{1,0:T(8,128)(2,1)S(1)} %get-tuple-element.92), channel_id=1, source_target_pairs={{0,64},{1,65},{2,66},{3,67},{4,68},{5,69},{6,70},{7,71},{8,72},{9,... | collective-permute-start | bytes 294920 | tf_op jit(solution)/shard_map/ppermute | solution.py:35
  212.3 6.7 %all-to-all-done.2 = bf16[8,8,6144]{2,1,0:T(8,128)(2,1)S(1)} async-done(((bf16[8,8,6144]{2,1,0:T(8,128)(2,1)}), bf16[8,8,6144]{2,1,0:T(8,128)(2,1)S(1)}, u32[]{:S(2)}, u32[]{:S(2)}) %all-to-all-start.2) | async-done | bytes 786464 | tf_op jit(solution)/shard_map/all_to_all | solution.py:577
  219.2 1.0 add_convert_fusion.5
  (99 shorter events, 6.0 us)
Async XLA Ops:
  0.0 0.8 copy-start.3
  0.8 0.8 copy-start.4
  1.5 0.7 copy-start.5
  2.2 0.7 copy-start.6
  3.2 9.2 %collective-permute-start = (bf16[144,256]{1,0:T(8,128)(2,1)S(1)}, bf16[144,256]{1,0:T(8,128)(2,1)S(1)}, u32[]{:S(2)}, u32[]{:S(2)}) collective-permute-start(bf16[144,256]{1,0:T(8,128)(2,1)S(1)} %shard_map.127), channel_id=1, source_target_pairs={{0,48},{1,49},{2,50},{3,51},{4,52},{5,53},{6,54},{7,55},{8,56},{9,... | collective-permute-start | bytes 221192 | tf_op jit(solution)/shard_map/ppermute | solution.py:43
  6.4 6.8 %collective-permute-start.1 = (bf16[144,256]{1,0:T(8,128)(2,1)S(1)}, bf16[144,256]{1,0:T(8,128)(2,1)S(1)}, u32[]{:S(2)}, u32[]{:S(2)}) collective-permute-start(bf16[144,256]{1,0:T(8,128)(2,1)S(1)} %shard_map.127), channel_id=1, source_target_pairs={{0,16},{1,17},{2,18},{3,19},{4,20},{5,21},{6,22},{7,23},{8,24},{9,... | collective-permute-start | bytes 221192 | tf_op jit(solution)/shard_map/ppermute | solution.py:43
  6.4 6.8 %collective-permute-start.2 = (bf16[144,256]{1,0:T(8,128)(2,1)S(1)}, bf16[144,256]{1,0:T(8,128)(2,1)S(1)}, u32[]{:S(2)}, u32[]{:S(2)}) collective-permute-start(bf16[144,256]{1,0:T(8,128)(2,1)S(1)} %shard_map.127), channel_id=1, source_target_pairs={{0,32},{1,33},{2,34},{3,35},{4,36},{5,37},{6,38},{7,39},{8,40},{9,... | collective-permute-start | bytes 221192 | tf_op jit(solution)/shard_map/ppermute | solution.py:43
  8.6 15.9 %collective-permute-start.4 = (bf16[768,384]{1,0:T(8,128)(2,1)}, bf16[768,384]{1,0:T(8,128)(2,1)S(1)}, u32[]{:S(2)}, u32[]{:S(2)}) collective-permute-start(bf16[768,384]{1,0:T(8,128)(2,1)} %param.19), channel_id=1, source_target_pairs={{0,48},{1,49},{2,50},{3,51},{4,52},{5,53},{6,54},{7,55},{8,56},{9,... | collective-permute-start | bytes 1769480 | tf_op jit(solution)/shard_map/ppermute | solution.py:43
  9.6 15.9 %collective-permute-start.5 = (bf16[768,384]{1,0:T(8,128)(2,1)}, bf16[768,384]{1,0:T(8,128)(2,1)S(1)}, u32[]{:S(2)}, u32[]{:S(2)}) collective-permute-start(bf16[768,384]{1,0:T(8,128)(2,1)} %param.19), channel_id=1, source_target_pairs={{0,16},{1,17},{2,18},{3,19},{4,20},{5,21},{6,22},{7,23},{8,24},{9,... | collective-permute-start | bytes 1769480 | tf_op jit(solution)/shard_map/ppermute | solution.py:43
  13.2 8.7 %collective-permute-start.3 = (bf16[4,144,256]{2,1,0:T(8,128)(2,1)S(1)}, bf16[4,144,256]{2,1,0:T(8,128)(2,1)S(1)}, u32[]{:S(2)}, u32[]{:S(2)}) collective-permute-start(bf16[4,144,256]{2,1,0:T(8,128)(2,1)S(1)} %pad_maximum_fusion), channel_id=1, source_target_pairs={{0,64},{1,65},{2,66},{3,67},{4,68},{5,69},{6,70},{7,71},{8,72},{9,... | collective-permute-start | bytes 884744 | tf_op jit(solution)/shard_map/ppermute | solution.py:35
  16.9 9.5 %copy-start.14 = (s32[16,2]{0,1:T(2,128)S(1)}, s32[16,2]{0,1:T(2,128)}, u32[]{:S(2)}) copy-start(s32[16,2]{0,1:T(2,128)} %param.24) | copy-start | bytes 388
  24.5 1.2 copy-start.8
  25.6 0.8 copy-start.9
  25.8 20.2 %collective-permute-start.7 = (bf16[768,1152]{1,0:T(8,128)(2,1)S(1)}, bf16[768,1152]{1,0:T(8,128)(2,1)S(1)}, u32[]{:S(2)}, u32[]{:S(2)}) collective-permute-start(bf16[768,1152]{1,0:T(8,128)(2,1)S(1)} %constant_dynamic-update-slice_fusion.5.near), channel_id=1, source_target_pairs={{0,8},{1,9},{2,10},{3,11},{4,12},{5,13},{6,14},{7,15},{8,0},{9,1},... | collective-permute-start | bytes 5308424 | tf_op jit(solution)/shard_map/ppermute | solution.py:39
  26.4 4.5 %collective-permute-start.6 = (bf16[8,144,256]{2,1,0:T(8,128)(2,1)}, bf16[8,144,256]{2,1,0:T(8,128)(2,1)}, u32[]{:S(2)}, u32[]{:S(2)}) collective-permute-start(bf16[8,144,256]{2,1,0:T(8,128)(2,1)} %constant_dynamic-update-slice_fusion.mine), channel_id=1, source_target_pairs={{0,8},{1,9},{2,10},{3,11},{4,12},{5,13},{6,14},{7,15},{8,0},{9,1},... | collective-permute-start | bytes 1769480 | tf_op jit(solution)/shard_map/ppermute | solution.py:39
  27.7 13.0 %copy-start.10 = (bf16[16,6144]{1,0:T(8,128)(2,1)S(1)}, bf16[16,6144]{1,0:T(8,128)(2,1)}, u32[]{:S(2)}) copy-start(bf16[16,6144]{1,0:T(8,128)(2,1)} %param.18) | copy-start | bytes 589828
  28.7 12.7 %collective-permute-start.10 = (bf16[384,384]{1,0:T(8,128)(2,1)S(1)}, bf16[384,384]{1,0:T(8,128)(2,1)S(1)}, u32[]{:S(2)}, u32[]{:S(2)}) collective-permute-start(bf16[384,384]{1,0:T(8,128)(2,1)S(1)} %slice.43), channel_id=1, source_target_pairs={{0,48},{1,49},{2,50},{3,51},{4,52},{5,53},{6,54},{7,55},{8,56},{9,... | collective-permute-start | bytes 884744 | tf_op jit(solution)/shard_map/ppermute | solution.py:43
  30.9 10.5 %collective-permute-start.9 = (bf16[384,384]{1,0:T(8,128)(2,1)S(1)}, bf16[384,384]{1,0:T(8,128)(2,1)S(1)}, u32[]{:S(2)}, u32[]{:S(2)}) collective-permute-start(bf16[384,384]{1,0:T(8,128)(2,1)S(1)} %slice.42), channel_id=1, source_target_pairs={{0,16},{1,17},{2,18},{3,19},{4,20},{5,21},{6,22},{7,23},{8,24},{9,... | collective-permute-start | bytes 884744 | tf_op jit(solution)/shard_map/ppermute | solution.py:43
  30.9 0.9 copy-start.7
  37.6 8.4 %collective-permute-start.8 = (bf16[128,768]{1,0:T(8,128)(2,1)S(1)}, bf16[128,768]{1,0:T(8,128)(2,1)S(1)}, u32[]{:S(2)}, u32[]{:S(2)}) collective-permute-start(bf16[128,768]{1,0:T(8,128)(2,1)S(1)} %shard_map.128.block), channel_id=1, source_target_pairs={{0,64},{1,65},{2,66},{3,67},{4,68},{5,69},{6,70},{7,71},{8,72},{9,... | collective-permute-start | bytes 589832 | tf_op jit(solution)/shard_map/ppermute | solution.py:35
  46.1 2.1 collective-permute-start.11
  48.2 34.0 %collective-permute-start.15 = (bf16[6144,512]{1,0:T(8,128)(2,1)}, bf16[6144,512]{1,0:T(8,128)(2,1)}, u32[]{:S(2)}, u32[]{:S(2)}) collective-permute-start(bf16[6144,512]{1,0:T(8,128)(2,1)} %bitcast.55), channel_id=1, source_target_pairs={{0,8},{1,9},{2,10},{3,11},{4,12},{5,13},{6,14},{7,15},{8,0},{9,1},... | collective-permute-start | bytes 18874376 | tf_op jit(solution)/shard_map/ppermute | solution.py:39
  48.3 33.9 %collective-permute-start.16 = (bf16[6144,512]{1,0:T(8,128)(2,1)}, bf16[6144,512]{1,0:T(8,128)(2,1)}, u32[]{:S(2)}, u32[]{:S(2)}) collective-permute-start(bf16[6144,512]{1,0:T(8,128)(2,1)} %bitcast.69), channel_id=1, source_target_pairs={{0,8},{1,9},{2,10},{3,11},{4,12},{5,13},{6,14},{7,15},{8,0},{9,1},... | collective-permute-start | bytes 18874376 | tf_op jit(solution)/shard_map/ppermute | solution.py:39
  48.7 96.8 %collective-permute-start.25 = (bf16[512,6144]{1,0:T(8,128)(2,1)}, bf16[512,6144]{1,0:T(8,128)(2,1)}, u32[]{:S(2)}, u32[]{:S(2)}) collective-permute-start(bf16[512,6144]{1,0:T(8,128)(2,1)} %bitcast.58), channel_id=1, source_target_pairs={{0,8},{1,9},{2,10},{3,11},{4,12},{5,13},{6,14},{7,15},{8,0},{9,1},... | collective-permute-start | bytes 18874376 | tf_op jit(solution)/shard_map/ppermute | solution.py:39
  51.7 9.6 %copy-start.11 = (bf16[16,3072]{1,0:T(8,128)(2,1)S(1)}, bf16[16,3072]{1,0:T(8,128)(2,1)}, u32[]{:S(2)}) copy-start(bf16[16,3072]{1,0:T(8,128)(2,1)} %get-tuple-element.57) | copy-start | bytes 294916
  51.7 29.3 %copy-start.2 = (bf16[16,3072]{1,0:T(8,128)(2,1)S(1)}, bf16[16,3072]{1,0:T(8,128)(2,1)}, u32[]{:S(2)}) copy-start(bf16[16,3072]{1,0:T(8,128)(2,1)} %get-tuple-element.93.res_own) | copy-start | bytes 294916
  51.8 29.3 %all-to-all-start = ((bf16[8,32,3072]{2,1,0:T(8,128)(2,1)}), bf16[8,32,3072]{2,1,0:T(8,128)(2,1)S(1)}, u32[]{:S(2)}, u32[]{:S(2)}) async-start(bf16[8,32,3072]{2,1,0:T(8,128)(2,1)} %shard_map.129), calls=%async_computation | async-start | bytes 3145728 | tf_op jit(solution)/shard_map/all_to_all | solution.py:513
  58.6 20.9 %collective-permute-start.13 = (s32[32]{0:T(128)S(1)}, s32[32]{0:T(128)S(1)}, u32[]{:S(2)}, u32[]{:S(2)}) collective-permute-start(s32[32]{0:T(128)S(1)} %reshape.31), channel_id=1, source_target_pairs={{0,64},{1,65},{2,66},{3,67},{4,68},{5,69},{6,70},{7,71},{8,72},{9,... | collective-permute-start | bytes 392 | tf_op jit(solution)/shard_map/ppermute | solution.py:35
  61.3 19.7 %collective-permute-start.12 = (bf16[16,3072]{1,0:T(8,128)(2,1)S(1)}, bf16[16,3072]{1,0:T(8,128)(2,1)S(1)}, u32[]{:S(2)}, u32[]{:S(2)}) collective-permute-start(bf16[16,3072]{1,0:T(8,128)(2,1)S(1)} %copy-done.11), channel_id=1, source_target_pairs={{0,64},{1,65},{2,66},{3,67},{4,68},{5,69},{6,70},{7,71},{8,72},{9,... | collective-permute-start | bytes 294920 | tf_op jit(solution)/shard_map/ppermute | solution.py:35
  99.1 33.8 %copy-start.12 = (bf16[6144]{0:T(1024)(128)(2,1)S(1)}, bf16[6144]{0:T(1024)(128)(2,1)}, u32[]{:S(2)}) copy-start(bf16[6144]{0:T(1024)(128)(2,1)} %param.20) | copy-start | bytes 36868
  99.1 33.8 %dynamic-slice-start = ((bf16[6144]{0:T(1024)(128)(2,1)}, s32[]{:T(128)}), bf16[3072]{0:T(1024)(128)(2,1)S(1)}, s32[]{:S(2)}) async-start(bf16[6144]{0:T(1024)(128)(2,1)} %param.20, s32[]{:T(128)} %select_n.82), calls=%async_computation.3 | async-start | bytes 12800 | tf_op jit(solution)/shard_map/dynamic-slice
  99.1 18.0 %collective-permute-start.20 = (bf16[128,3072]{1,0:T(8,128)(2,1)S(1)}, bf16[128,3072]{1,0:T(8,128)(2,1)S(1)}, u32[]{:S(2)}, u32[]{:S(2)}) collective-permute-start(bf16[128,3072]{1,0:T(8,128)(2,1)S(1)} %bitcast.61), channel_id=1, source_target_pairs={{0,16},{1,17},{2,18},{3,19},{4,20},{5,21},{6,22},{7,23},{8,24},{9,... | collective-permute-start | bytes 2359304 | tf_op jit(solution)/shard_map/ppermute | solution.py:43
  99.7 17.6 %collective-permute-start.22 = (bf16[128,3072]{1,0:T(8,128)(2,1)S(1)}, bf16[128,3072]{1,0:T(8,128)(2,1)S(1)}, u32[]{:S(2)}, u32[]{:S(2)}) collective-permute-start(bf16[128,3072]{1,0:T(8,128)(2,1)S(1)} %bitcast.62), channel_id=1, source_target_pairs={{0,48},{1,49},{2,50},{3,51},{4,52},{5,53},{6,54},{7,55},{8,56},{9,... | collective-permute-start | bytes 2359304 | tf_op jit(solution)/shard_map/ppermute | solution.py:43
  102.3 18.3 %collective-permute-start.17 = (bf16[128,3072]{1,0:T(8,128)(2,1)S(1)}, bf16[128,3072]{1,0:T(8,128)(2,1)S(1)}, u32[]{:S(2)}, u32[]{:S(2)}) collective-permute-start(bf16[128,3072]{1,0:T(8,128)(2,1)S(1)} %bitcast.63), channel_id=1, source_target_pairs={{0,64},{1,65},{2,66},{3,67},{4,68},{5,69},{6,70},{7,71},{8,72},{9,... | collective-permute-start | bytes 2359304 | tf_op jit(solution)/shard_map/ppermute | solution.py:35
  117.2 13.3 %collective-permute-start.21 = (bf16[64,3072]{1,0:T(8,128)(2,1)S(1)}, bf16[64,3072]{1,0:T(8,128)(2,1)S(1)}, u32[]{:S(2)}, u32[]{:S(2)}) collective-permute-start(bf16[64,3072]{1,0:T(8,128)(2,1)S(1)} %slice.56), channel_id=1, source_target_pairs={{0,16},{1,17},{2,18},{3,19},{4,20},{5,21},{6,22},{7,23},{8,24},{9,... | collective-permute-start | bytes 1179656 | tf_op jit(solution)/shard_map/ppermute | solution.py:43
  117.3 13.2 %collective-permute-start.23 = (bf16[64,3072]{1,0:T(8,128)(2,1)S(1)}, bf16[64,3072]{1,0:T(8,128)(2,1)S(1)}, u32[]{:S(2)}, u32[]{:S(2)}) collective-permute-start(bf16[64,3072]{1,0:T(8,128)(2,1)S(1)} %slice.57), channel_id=1, source_target_pairs={{0,48},{1,49},{2,50},{3,51},{4,52},{5,53},{6,54},{7,55},{8,56},{9,... | collective-permute-start | bytes 1179656 | tf_op jit(solution)/shard_map/ppermute | solution.py:43
  120.6 24.9 %collective-permute-start.18 = (bf16[128,3072]{1,0:T(8,128)(2,1)S(1)}, bf16[128,3072]{1,0:T(8,128)(2,1)S(1)}, u32[]{:S(2)}, u32[]{:S(2)}) collective-permute-start(bf16[128,3072]{1,0:T(8,128)(2,1)S(1)} %collective-permute-done.17.near), channel_id=1, source_target_pairs={{0,48},{1,49},{2,50},{3,51},{4,52},{5,53},{6,54},{7,55},{8,56},{9,... | collective-permute-start | bytes 2359304 | tf_op jit(solution)/shard_map/ppermute | solution.py:43
  121.8 23.7 %collective-permute-start.19 = (bf16[128,3072]{1,0:T(8,128)(2,1)S(1)}, bf16[128,3072]{1,0:T(8,128)(2,1)S(1)}, u32[]{:S(2)}, u32[]{:S(2)}) collective-permute-start(bf16[128,3072]{1,0:T(8,128)(2,1)S(1)} %collective-permute-done.17.near), channel_id=1, source_target_pairs={{0,16},{1,17},{2,18},{3,19},{4,20},{5,21},{6,22},{7,23},{8,24},{9,... | collective-permute-start | bytes 2359304 | tf_op jit(solution)/shard_map/ppermute | solution.py:43
  130.6 15.0 %collective-permute-start.24 = (bf16[128,3072]{1,0:T(8,128)(2,1)S(1)}, bf16[128,3072]{1,0:T(8,128)(2,1)S(1)}, u32[]{:S(2)}, u32[]{:S(2)}) collective-permute-start(bf16[128,3072]{1,0:T(8,128)(2,1)S(1)} %constant_dynamic-update-slice_fusion.10.far), channel_id=1, source_target_pairs={{0,64},{1,65},{2,66},{3,67},{4,68},{5,69},{6,70},{7,71},{8,72},{9,... | collective-permute-start | bytes 2359304 | tf_op jit(solution)/shard_map/ppermute | solution.py:35
  133.0 2.8 %copy-start = (bf16[1,6144,512]{2,1,0:T(8,128)(2,1)S(1)}, bf16[1,6144,512]{2,1,0:T(8,128)(2,1)}, u32[]{:S(2)}) copy-start(bf16[1,6144,512]{2,1,0:T(8,128)(2,1)} %param.21) | copy-start | bytes 18874372
  145.5 16.6 %copy-start.13 = (f32[16,2]{0,1:T(2,128)S(1)}, f32[16,2]{0,1:T(2,128)}, u32[]{:S(2)}) copy-start(f32[16,2]{0,1:T(2,128)} %param.25) | copy-start | bytes 388
  160.5 16.2 %collective-permute-start.29 = (bf16[64,6144]{1,0:T(8,128)(2,1)}, bf16[64,6144]{1,0:T(8,128)(2,1)}, u32[]{:S(2)}, u32[]{:S(2)}) collective-permute-start(bf16[64,6144]{1,0:T(8,128)(2,1)} %get-tuple-element.82), channel_id=1, source_target_pairs={{0,64},{1,65},{2,66},{3,67},{4,68},{5,69},{6,70},{7,71},{8,72},{9,... | collective-permute-start | bytes 2359304 | tf_op jit(solution)/shard_map/ppermute | solution.py:35
  162.2 18.0 %collective-permute-start.26 = (bf16[64,6144]{1,0:T(8,128)(2,1)S(1)}, bf16[64,6144]{1,0:T(8,128)(2,1)S(1)}, u32[]{:S(2)}, u32[]{:S(2)}) collective-permute-start(bf16[64,6144]{1,0:T(8,128)(2,1)S(1)} %get-tuple-element.75), channel_id=1, source_target_pairs={{0,16},{1,17},{2,18},{3,19},{4,20},{5,21},{6,22},{7,23},{8,24},{9,... | collective-permute-start | bytes 2359304 | tf_op jit(solution)/shard_map/ppermute | solution.py:43
  162.9 17.2 %collective-permute-start.27 = (bf16[64,6144]{1,0:T(8,128)(2,1)S(1)}, bf16[64,6144]{1,0:T(8,128)(2,1)S(1)}, u32[]{:S(2)}, u32[]{:S(2)}) collective-permute-start(bf16[64,6144]{1,0:T(8,128)(2,1)S(1)} %get-tuple-element.76), channel_id=1, source_target_pairs={{0,48},{1,49},{2,50},{3,51},{4,52},{5,53},{6,54},{7,55},{8,56},{9,... | collective-permute-start | bytes 2359304 | tf_op jit(solution)/shard_map/ppermute | solution.py:43
  165.9 2.8 %copy-start.1 = (bf16[1,512,6144]{2,1,0:T(8,128)(2,1)S(1)}, bf16[1,512,6144]{2,1,0:T(8,128)(2,1)}, u32[]{:S(2)}) copy-start(bf16[1,512,6144]{2,1,0:T(8,128)(2,1)} %param.23) | copy-start | bytes 18874372
  178.0 12.1 %collective-permute-start.32 = (bf16[64,3072]{1,0:T(8,128)(2,1)S(1)}, bf16[64,3072]{1,0:T(8,128)(2,1)S(1)}, u32[]{:S(2)}, u32[]{:S(2)}) collective-permute-start(bf16[64,3072]{1,0:T(8,128)(2,1)S(1)} %get-tuple-element.89), channel_id=1, source_target_pairs={{0,48},{1,49},{2,50},{3,51},{4,52},{5,53},{6,54},{7,55},{8,56},{9,... | collective-permute-start | bytes 1179656 | tf_op jit(solution)/shard_map/ppermute | solution.py:43
  179.8 13.4 %collective-permute-start.30 = (bf16[64,3072]{1,0:T(8,128)(2,1)S(1)}, bf16[64,3072]{1,0:T(8,128)(2,1)S(1)}, u32[]{:S(2)}, u32[]{:S(2)}) collective-permute-start(bf16[64,3072]{1,0:T(8,128)(2,1)S(1)} %get-tuple-element.90), channel_id=1, source_target_pairs={{0,16},{1,17},{2,18},{3,19},{4,20},{5,21},{6,22},{7,23},{8,24},{9,... | collective-permute-start | bytes 1179656 | tf_op jit(solution)/shard_map/ppermute | solution.py:43
  180.4 22.0 %collective-permute-start.28 = (bf16[64,6144]{1,0:T(8,128)(2,1)S(1)}, bf16[64,6144]{1,0:T(8,128)(2,1)S(1)}, u32[]{:S(2)}, u32[]{:S(2)}) collective-permute-start(bf16[64,6144]{1,0:T(8,128)(2,1)S(1)} %add_convert_fusion), channel_id=1, source_target_pairs={{0,64},{1,65},{2,66},{3,67},{4,68},{5,69},{6,70},{7,71},{8,72},{9,... | collective-permute-start | bytes 2359304 | tf_op jit(solution)/shard_map/ppermute | solution.py:35
  182.5 19.9 %collective-permute-start.34 = (bf16[64,3072]{1,0:T(8,128)(2,1)S(1)}, bf16[64,3072]{1,0:T(8,128)(2,1)S(1)}, u32[]{:S(2)}, u32[]{:S(2)}) collective-permute-start(bf16[64,3072]{1,0:T(8,128)(2,1)S(1)} %get-tuple-element.85), channel_id=1, source_target_pairs={{0,48},{1,49},{2,50},{3,51},{4,52},{5,53},{6,54},{7,55},{8,56},{9,... | collective-permute-start | bytes 1179656 | tf_op jit(solution)/shard_map/ppermute | solution.py:43
  185.4 17.0 %collective-permute-start.35 = (bf16[64,3072]{1,0:T(8,128)(2,1)S(1)}, bf16[64,3072]{1,0:T(8,128)(2,1)S(1)}, u32[]{:S(2)}, u32[]{:S(2)}) collective-permute-start(bf16[64,3072]{1,0:T(8,128)(2,1)S(1)} %get-tuple-element.87), channel_id=1, source_target_pairs={{0,16},{1,17},{2,18},{3,19},{4,20},{5,21},{6,22},{7,23},{8,24},{9,... | collective-permute-start | bytes 1179656 | tf_op jit(solution)/shard_map/ppermute | solution.py:43
  190.2 10.4 %collective-permute-start.33 = (bf16[64,3072]{1,0:T(8,128)(2,1)S(1)}, bf16[64,3072]{1,0:T(8,128)(2,1)S(1)}, u32[]{:S(2)}, u32[]{:S(2)}) collective-permute-start(bf16[64,3072]{1,0:T(8,128)(2,1)S(1)} %add_convert_fusion.1), channel_id=1, source_target_pairs={{0,48},{1,49},{2,50},{3,51},{4,52},{5,53},{6,54},{7,55},{8,56},{9,... | collective-permute-start | bytes 1179656 | tf_op jit(solution)/shard_map/ppermute | solution.py:43
  193.3 9.1 %collective-permute-start.31 = (bf16[64,3072]{1,0:T(8,128)(2,1)S(1)}, bf16[64,3072]{1,0:T(8,128)(2,1)S(1)}, u32[]{:S(2)}, u32[]{:S(2)}) collective-permute-start(bf16[64,3072]{1,0:T(8,128)(2,1)S(1)} %add_convert_fusion.3), channel_id=1, source_target_pairs={{0,16},{1,17},{2,18},{3,19},{4,20},{5,21},{6,22},{7,23},{8,24},{9,... | collective-permute-start | bytes 1179656 | tf_op jit(solution)/shard_map/ppermute | solution.py:43
  203.7 15.3 %all-to-all-start.2 = ((bf16[8,8,6144]{2,1,0:T(8,128)(2,1)}), bf16[8,8,6144]{2,1,0:T(8,128)(2,1)S(1)}, u32[]{:S(2)}, u32[]{:S(2)}) async-start(bf16[8,8,6144]{2,1,0:T(8,128)(2,1)} %bitcast.35), calls=%async_computation.2 | async-start | bytes 1572864 | tf_op jit(solution)/shard_map/all_to_all | solution.py:577
  209.5 9.7 %collective-permute-start.14 = (bf16[16,3072]{1,0:T(8,128)(2,1)S(1)}, bf16[16,3072]{1,0:T(8,128)(2,1)S(1)}, u32[]{:S(2)}, u32[]{:S(2)}) collective-permute-start(bf16[16,3072]{1,0:T(8,128)(2,1)S(1)} %get-tuple-element.92), channel_id=1, source_target_pairs={{0,64},{1,65},{2,66},{3,67},{4,68},{5,69},{6,70},{7,71},{8,72},{9,... | collective-permute-start | bytes 294920 | tf_op jit(solution)/shard_map/ppermute | solution.py:35
